TPU v7x, 256 devices: a whole 4x4x8 slice. The times are simulated.
256 devices in a mesh: tm: 32 (over y, z), azi: 2 (over x_hi), rad: 4 (over x_lo, core).
Axes of the slice: x: 4 (x_hi: 2, x_lo: 2; x = x_hi * 2 + x_lo), y: 4, z: 8, core: 2. Of those that a mesh axis runs over, the one named last changes fastest.
Arguments:
- start_states: float32 [32, 64, 32, 128], P('tm', 'rad', 'azi'), may hold values from -6 to 6
- target: float32 [32, 64, 32, 128], P('tm', 'rad', 'azi'), may hold values from -6 to 6
- conductivity: float32 [64, 32, 128], P('rad', 'azi'), may hold values from 0.1 to 1000
- material: int32 [64, 32, 128], P('rad', 'azi'), may hold values from 0 to 2
- current: float32 [64, 32, 128], P('rad', 'azi'), may hold values from -6 to 6
- bh_coef: float32 [3], replicated, may hold values from 0.05 to 0.5
Outputs:
- new_end: float32 [32, 64, 32, 128], P('tm', 'rad', 'azi')
- grad_conductivity: float32 [64, 32, 128], P('rad', 'azi')
- bh_grad: float32 [3], replicated
Inputs may be any that keep to these rules, and one draw needn't show every extreme that they name: `material`: 0 marks air, 1 iron, 2 copper.
All inputs are finite; a program needn't handle non-finite values.
Results may differ from a plain program's by a relative error of at most 0.00011.
Values sent between devices are 32-bit elements; how exact they have to be, the bound alone decides.
No kernel may reach another device: no remote copies, remote signals or barrier semaphores. Data moves between devices by JAX's collectives and lax.ppermute only.
A program may use at most 64 MiB of HBM per device.

v0:
```python
import math

import jax
import jax.numpy as jnp
from jax import lax
from jax.sharding import PartitionSpec as P

STEPS = 2
SWEEPS = 8


DT_FINE = 0.25
LOWER_EDGE = 0.05
UPPER_EDGE = 1.95


def with_halo(value, sides, width):
    for axis, dim in sides:
        devices, length = (lax.axis_size(axis), value.shape[dim])
        up = [(i, (i + 1) % devices) for i in range(devices - 1)]
        down = [(j, i) for i, j in up]
        last = lax.slice_in_dim(value, length - width, length, axis=dim)
        leading = lax.slice_in_dim(value, 0, width, axis=dim)
        before = lax.ppermute(last, axis, up)
        after = lax.ppermute(leading, axis, down)
        value = jnp.concatenate([before, value, after], axis=dim)
    return value


def shifted(value, axis, by):
    devices = lax.axis_size(axis)
    pairs = [(i, i + by) for i in range(devices) if 0 <= i + by < devices]
    return lax.ppermute(value, axis, pairs)


def prefix(value, axis, join, neutral):
    count, mine = (lax.axis_size(axis), lax.axis_index(axis))
    pieces = jax.tree.map(lambda part: lax.all_gather(part, axis), value)
    pieces = jax.tree.map(lambda part: part[::-1], pieces)
    mine = count - 1 - mine
    total = jax.tree.map(
        lambda part, zero: jnp.full_like(part, 0) + jnp.asarray(zero, part.dtype), value, neutral
    )

    def step(position, total):
        longer = join(total, jax.tree.map(lambda part: part[position], pieces))
        return jax.tree.map(lambda new, old: jnp.where(position < mine, new, old), longer, total)

    return lax.fori_loop(0, count - 1, step, total)


def square_field(extended):
    radial = 0.5 * (extended[2:, 1:-1] - extended[:-2, 1:-1])
    azimuthal = 0.5 * (extended[1:-1, 2:] - extended[1:-1, :-2])
    return radial * radial + azimuthal * azimuthal


def reluctance(bsquare, mat_ext, bh_coef):
    saturation = bsquare / (1.0 + bsquare)
    iron_value = bh_coef[2] + bh_coef[0] * jnp.exp(bh_coef[1] * saturation)
    return (jnp.where(mat_ext == 1, iron_value, 1.0), saturation)


def face_terms(reluct_ext):
    centre = reluct_ext[1:-1, 1:-1]
    axial = jnp.pad(centre, ((0, 0), (0, 0), (1, 1)), constant_values=1.0)
    return (
        0.5 * (centre + reluct_ext[2:, 1:-1]),
        0.5 * (centre + reluct_ext[:-2, 1:-1]),
        0.5 * (centre + reluct_ext[1:-1, 2:]),
        0.5 * (centre + reluct_ext[1:-1, :-2]),
        0.5 * (centre + axial[:, :, 2:]),
        0.5 * (centre + axial[:, :, :-2]),
    )


def apply_operator(extended, face_list, mass_term):
    centre = extended[1:-1, 1:-1]
    axial = jnp.pad(centre, ((0, 0), (0, 0), (1, 1)))
    neighbours = (
        extended[2:, 1:-1],
        extended[:-2, 1:-1],
        extended[1:-1, 2:],
        extended[1:-1, :-2],
        axial[:, :, 2:],
        axial[:, :, :-2],
    )
    result = mass_term * centre
    for face, beside in zip(face_list, neighbours):
        result = result + face * (centre - beside)
    return result


def implicit_step(start_field, extended, mat_ext, mass_term, forcing, bh_coef, widen):
    reluct_ext, saturation = reluctance(square_field(extended), mat_ext, bh_coef)
    face_list = face_terms(reluct_ext)
    diagonal = mass_term
    for face in face_list:
        diagonal = diagonal + face
    inverse = 1.0 / diagonal
    theta = 0.5 * (UPPER_EDGE + LOWER_EDGE)
    delta = 0.5 * (UPPER_EDGE - LOWER_EDGE)
    scaled = theta / delta
    ratio = 1.0 / scaled
    residual = (
        mass_term * start_field
        + forcing
        - apply_operator(extended[1:-1, 1:-1], face_list, mass_term)
    )
    direction = residual * inverse / theta
    iterate = start_field
    for sweep_index in range(SWEEPS):
        iterate = iterate + direction
        if sweep_index < SWEEPS - 1:
            residual = residual - apply_operator(widen(direction), face_list, mass_term)
            following = 1.0 / (2.0 * scaled - ratio)
            direction = following * ratio * direction + 2.0 * following / delta * residual * inverse
            ratio = following
    return (iterate, reluct_ext[1:-1, 1:-1], saturation[1:-1, 1:-1])


def coarse_factor(conductivity, reluct_zero, dt_coarse):
    lumped = 6.0 * reluct_zero
    return (conductivity / (conductivity + dt_coarse * lumped), lumped)


def gradient_terms(slope, jump, conductivity, lumped, dt_coarse, iron, saturation, bh_coef):
    weight = slope * jump
    denom = conductivity + dt_coarse * lumped
    denom_sq = denom * denom
    grad_cond = weight * (dt_coarse * lumped) / denom_sq
    hterm = 6.0 * weight * (-dt_coarse * conductivity) / denom_sq * iron
    growth = jnp.exp(bh_coef[1] * saturation)
    coef_part = jnp.stack(
        [jnp.sum(hterm * growth), jnp.sum(hterm * bh_coef[0] * saturation * growth), jnp.sum(hterm)]
    )
    return (grad_cond, coef_part)


def widen_one(values):
    return with_halo(values, (("azi", 1), ("rad", 0)), 1)


def widen_two(values):
    return with_halo(values, (("azi", 1), ("rad", 0)), 2)


def compose(earlier, later):
    return (earlier[0] * later[0], later[0] * earlier[1] + later[1])


def local(start_states, target, conductivity, material, current, bh_coef):
    position = lax.axis_index("tm")
    slices = lax.axis_size("tm")
    old_start = start_states[0]
    target_field = target[0]
    mass_term = conductivity / DT_FINE
    mat_ext = with_halo(material, (("azi", 1), ("rad", 0)), 1)
    source = current * (material == 2).astype(jnp.float32)
    iron = (material == 1).astype(jnp.float32)
    angular = 4.0 * math.pi / (slices * STEPS)
    dt_coarse = STEPS * DT_FINE
    slice_pos = position.astype(jnp.float32)
    fine_end = old_start
    reluct_zero = None
    saturation_zero = None
    for step_index in range(STEPS):
        extended = widen_two(fine_end)
        forcing = source * jnp.cos(angular * (slice_pos * STEPS + (step_index + 1)))
        fine_end, reluct_now, saturation_now = implicit_step(
            fine_end, extended, mat_ext, mass_term, forcing, bh_coef, widen_one
        )
        if step_index == 0:
            reluct_zero = reluct_now
            saturation_zero = saturation_now
    factor, lumped = coarse_factor(conductivity, reluct_zero, dt_coarse)
    identity = (jnp.ones_like(factor), jnp.zeros_like(factor))

    def hand_over(turn, begin):
        outgoing = fine_end + factor * (begin - old_start)
        incoming = shifted(outgoing, "tm", 1)
        return jnp.where(position == turn + 1, incoming, begin)

    begin = lax.fori_loop(0, slices - 1, hand_over, old_start)
    jump = begin - old_start
    end_field = fine_end + factor * jump
    resid = end_field - target_field
    ignored, tail = prefix((factor, factor * resid), "tm", compose, identity)
    slope = resid + tail
    grad_local, coef_local = gradient_terms(
        slope, jump, conductivity, lumped, dt_coarse, iron, saturation_zero, bh_coef
    )
    grad_sum = lax.psum(grad_local, "tm")
    coef_sum = lax.psum(coef_local, ("tm", "azi", "rad"))
    count = (
        slices
        * old_start.shape[0]
        * old_start.shape[1]
        * old_start.shape[2]
        * lax.axis_size("azi")
        * lax.axis_size("rad")
    )
    return (end_field[None], grad_sum, coef_sum / count)


def solution(mesh):
    placed = (
        P("tm", "rad", "azi", None),
        P("tm", "rad", "azi", None),
        P("rad", "azi", None),
        P("rad", "azi", None),
        P("rad", "azi", None),
        P(),
    )
    return jax.shard_map(
        local,
        mesh=mesh,
        in_specs=placed,
        out_specs=(P("tm", "rad", "azi", None), P("rad", "azi", None), P()),
        check_vma=False,
    )
```

profile of v0, /device:TPU:1, one launch (start us, length us, event | category | flops | bytes accessed | tf_op | source)
XLA Modules:
  0.0 921.8 jit_solution(18308090933054593579)
XLA Ops:
  8.1 5.5 collective-permute-start.5
  15.8 5.5 collective-permute-start.1
  46.3 6.4 collective-permute-start.9
  60.1 5.2 collective-permute-start.13
  66.6 4.6 collective-permute-done.14
  73.2 4.9 collective-permute-start.16
  82.5 4.6 collective-permute-done.18
  89.0 5.0 collective-permute-start.20
  98.4 4.6 collective-permute-done.22
  104.9 5.0 collective-permute-start.24
  114.3 4.6 collective-permute-done.26
  120.8 5.0 collective-permute-start.28
  130.3 4.6 collective-permute-done.30
  136.8 5.0 collective-permute-start.32
  146.2 4.6 collective-permute-done.34
  152.8 5.0 collective-permute-start.36
  162.4 4.7 collective-permute-done.38
  169.0 5.0 collective-permute-start.40
  180.8 4.6 collective-permute-done.42
  187.3 5.0 collective-permute-start.44
  196.7 4.6 collective-permute-done.46
  203.2 5.0 collective-permute-start.48
  212.5 4.6 collective-permute-done.50
  219.1 5.0 collective-permute-start.52
  228.4 4.6 collective-permute-done.54
  234.9 5.0 collective-permute-start.56
  244.5 4.6 collective-permute-done.58
  251.0 5.0 collective-permute-start.60
  260.4 4.6 collective-permute-done.62
  266.9 5.0 collective-permute-start.64
  283.0 5.0 collective-permute-start.68
  289.3 239.3 %while.27 = (s32[]{:T(128)}, f32[16,16,128]{2,1,0:T(8,128)S(1)}, s32[]{:T(128)}, f32[16,16,128]{2,1,0:T(8,128)S(1)}, f32[16,16,128]{2,1,0:T(8,128)S(1)}, /*index=5*/f32[16,16,128]{2,1,0:T(8,128)S(1)}, s32[]{:T(128)}) while((s32[]{:T(128)}, f32[16,16,128]{2,1,0:T(8,128)S(1)}, s32[]{:T(128)}, f32[16,16,128]{2,1,0:T(8,128)S(1)}, ...), condition=%wide.region_1.2_spmd, body=%wide.region_0.1_spmd.sunk | while | flops 131075 | bytes 1572991 | solution.py:184
  315.6 4.9 collective-permute-start
  322.9 5.2 collective-permute-start
  330.0 5.3 collective-permute-start
  337.3 5.9 collective-permute-start
  347.1 6.0 collective-permute-start
  357.6 6.2 collective-permute-start
  363.7 4.8 collective-permute-done
  375.0 5.4 collective-permute-start
  383.5 5.1 collective-permute-start
  391.3 4.9 collective-permute-start
  404.8 5.3 collective-permute-start
  412.1 5.4 collective-permute-start
  419.6 5.0 collective-permute-start
  426.6 5.0 collective-permute-start
  433.8 5.3 collective-permute-start
  442.4 5.0 collective-permute-start
  449.6 5.0 collective-permute-start
  456.6 4.7 collective-permute-start
  463.3 5.4 collective-permute-start
  470.7 6.7 collective-permute-start
  479.5 5.5 collective-permute-start
  487.0 5.6 collective-permute-start
  494.6 6.2 collective-permute-start
  502.8 6.0 collective-permute-start
  511.9 6.6 collective-permute-start
  521.2 5.4 collective-permute-start
  529.4 4.7 rev.6
  534.1 125.6 %all-gather.7.cloned.1.call-done = f32[512,16,128]{2,1,0:T(8,128)} async-done(((f32[16,16,128]{2,1,0:T(8,128)}), f32[512,16,128]{2,1,0:T(8,128)}) %all-gather.7.cloned.1.call-update) | async-done | bytes 4194320 | tf_op jit(solution)/shard_map/all_gather | solution.py:38
  659.7 4.7 rev.7
  664.4 34.0 %while.28 = (s32[]{:T(128)}, f32[16,16,128]{2,1,0:T(8,128)S(1)}, s32[]{:T(128)}, f32[32,16,16,128]{3,2,1,0:T(8,128)}, f32[32,16,16,128]{3,2,1,0:T(8,128)}, /*index=5*/s32[]{:T(128)}, s32[]{:T(128)}) while((s32[]{:T(128)}, f32[16,16,128]{2,1,0:T(8,128)S(1)}, s32[]{:T(128)}, f32[32,16,16,128]{3,2,1,0:T(8,128)}, ...), condition=%wide.region_3.4_spmd.clone, body=%wide.region_2.3_spmd.clone.sunk | while | flops 131076 | bytes 524389 | solution.py:49
  702.4 77.7 %psum.15 = f32[3]{0:T(128)S(1)} all-reduce(f32[3]{0:T(128)S(1)} %pad_maximum_fusion.168), channel_id=1, replica_groups=mesh['tm'=32,'azi'=2,'rad'=4] {'tm','azi','rad'}, use_global_device_ids=true, to_apply=%region_8.9 | all-reduce | flops 3 | bytes 24 | tf_op jit(solution)/shard_map/psum | solution.py:194
  781.3 132.3 %all-reduce.20.cloned.1.call-done = f32[16,16,128]{2,1,0:T(8,128)} async-done(((f32[16,16,128]{2,1,0:T(8,128)}), f32[16,16,128]{2,1,0:T(8,128)}) %all-reduce.20.cloned.1.call-update) | async-done | bytes 131088 | tf_op jit(solution)/shard_map/psum | solution.py:193
  (323 shorter events, 265.3 us)
Async XLA Ops:
  7.2 522.2 %all-gather.5.cloned.1.call-start = ((), (), s32[]{:S(2)}) async-start(), calls=%async_computation.1 | async-start | bytes 4325376 | tf_op jit(solution)/shard_map/all_gather | solution.py:38
  8.1 16.0 %collective-permute-start.5 = (f32[16,2,128]{2,1,0:T(2,128)S(1)}, f32[16,2,128]{2,1,0:T(2,128)S(1)}, u32[]{:S(2)}, u32[]{:S(2)}) collective-permute-start(f32[16,2,128]{2,1,0:T(2,128)S(1)} %get-tuple-element.365), channel_id=1, source_target_pairs={{0,4},{1,5},{2,6},{3,7},{8,12},{9,13},{10,14},{11,15},{16,20},{17,... | collective-permute-start | bytes 49160 | tf_op jit(solution)/shard_map/ppermute | solution.py:24
  13.6 10.5 %collective-permute-start.6 = (f32[16,2,128]{2,1,0:T(2,128)S(1)}, f32[16,2,128]{2,1,0:T(2,128)S(1)}, u32[]{:S(2)}, u32[]{:S(2)}) collective-permute-start(f32[16,2,128]{2,1,0:T(2,128)S(1)} %get-tuple-element.366), channel_id=1, source_target_pairs={{4,0},{5,1},{6,2},{7,3},{12,8},{13,9},{14,10},{15,11},{20,16},{21,... | collective-permute-start | bytes 49160 | tf_op jit(solution)/shard_map/ppermute | solution.py:25
  15.8 14.6 %collective-permute-start.1 = (s32[16,1,128]{2,1,0:T(1,128)S(1)}, s32[16,1,128]{2,1,0:T(1,128)S(1)}, u32[]{:S(2)}, u32[]{:S(2)}) collective-permute-start(s32[16,1,128]{2,1,0:T(1,128)S(1)} %get-tuple-element.367), channel_id=1, source_target_pairs={{0,4},{1,5},{2,6},{3,7},{8,12},{9,13},{10,14},{11,15},{16,20},{17,... | collective-permute-start | bytes 24584 | tf_op jit(solution)/shard_map/ppermute | solution.py:24
  21.3 9.2 collective-permute-start.2
  24.9 10.7 %collective-permute-start.7 = (f32[2,20,128]{2,1,0:T(8,128)S(1)}, f32[2,20,128]{2,1,0:T(8,128)S(1)}, u32[]{:S(2)}, u32[]{:S(2)}) collective-permute-start(f32[2,20,128]{2,1,0:T(8,128)S(1)} %get-tuple-element.304), channel_id=1, source_target_pairs={{1,0},{2,1},{3,2},{5,4},{6,5},{7,6},{9,8},{10,9},{11,10},{13,12},{... | collective-permute-start | bytes 61448 | tf_op jit(solution)/shard_map/ppermute | solution.py:25
  28.3 7.2 collective-permute-start.8
  31.2 6.3 collective-permute-start.3
  45.0 7.7 collective-permute-start.10
  46.3 7.2 collective-permute-start.9
  60.1 6.5 collective-permute-start.13
  65.3 5.9 collective-permute-start.14
  71.2 7.0 collective-permute-start.15
  81.2 5.9 collective-permute-start.18
  87.1 7.0 collective-permute-start.19
  97.1 5.9 collective-permute-start.22
  103.0 7.0 collective-permute-start.23
  112.9 5.9 collective-permute-start.26
  118.9 7.0 collective-permute-start.27
  134.9 7.0 collective-permute-start.31
  150.8 7.0 collective-permute-start.35
  161.0 6.0 collective-permute-start.38
  167.0 7.0 collective-permute-start.39
  169.0 6.0 collective-permute-start.40
  185.4 7.0 collective-permute-start.43
  201.3 7.0 collective-permute-start.47
  217.1 7.0 collective-permute-start.51
  233.0 7.0 collective-permute-start.55
  249.1 7.0 collective-permute-start.59
  265.0 7.0 collective-permute-start.63
  275.0 6.0 collective-permute-start.66
  281.1 7.1 collective-permute-start.67
  288.1 371.7 %all-gather.7.cloned.1.call-start = ((), (), s32[]{:S(2)}) async-start(), calls=%async_computation.2 | async-start | bytes 4325376 | tf_op jit(solution)/shard_map/all_gather | solution.py:38
  294.9 6.1 collective-permute-start
  301.1 7.7 collective-permute-start
  308.8 6.7 collective-permute-start
  315.6 7.1 collective-permute-start
  322.9 7.1 collective-permute-start
  330.0 7.2 collective-permute-start
  337.3 9.7 %collective-permute-start = (f32[16,16,128]{2,1,0:T(8,128)S(1)}, f32[16,16,128]{2,1,0:T(8,128)S(1)}, u32[]{:S(2)}, u32[]{:S(2)}) collective-permute-start(f32[16,16,128]{2,1,0:T(8,128)S(1)} %multiply_add_fusion.16), channel_id=1, source_target_pairs={{0,8},{8,16},{16,24},{24,32},{32,40},{40,48},{48,56},{56,64},{64,7... | collective-permute-start | bytes 393224 | tf_op jit(solution)/shard_map/while/body/eval_jaxpr/ppermute | solution.py:33
  347.1 10.3 %collective-permute-start = (f32[16,16,128]{2,1,0:T(8,128)S(1)}, f32[16,16,128]{2,1,0:T(8,128)S(1)}, u32[]{:S(2)}, u32[]{:S(2)}) collective-permute-start(f32[16,16,128]{2,1,0:T(8,128)S(1)} %multiply_add_fusion.16), channel_id=1, source_target_pairs={{0,8},{8,16},{16,24},{24,32},{32,40},{40,48},{48,56},{56,64},{64,7... | collective-permute-start | bytes 393224 | tf_op jit(solution)/shard_map/while/body/eval_jaxpr/ppermute | solution.py:33
  357.6 11.0 %collective-permute-start = (f32[16,16,128]{2,1,0:T(8,128)S(1)}, f32[16,16,128]{2,1,0:T(8,128)S(1)}, u32[]{:S(2)}, u32[]{:S(2)}) collective-permute-start(f32[16,16,128]{2,1,0:T(8,128)S(1)} %multiply_add_fusion.16), channel_id=1, source_target_pairs={{0,8},{8,16},{16,24},{24,32},{32,40},{40,48},{48,56},{56,64},{64,7... | collective-permute-start | bytes 393224 | tf_op jit(solution)/shard_map/while/body/eval_jaxpr/ppermute | solution.py:33
  368.6 6.3 collective-permute-start
  375.0 8.4 collective-permute-start
  383.5 7.8 collective-permute-start
  391.3 6.9 collective-permute-start
  398.3 6.4 collective-permute-start
  404.8 7.3 collective-permute-start
  412.1 7.4 collective-permute-start
  419.6 6.9 collective-permute-start
  426.6 7.1 collective-permute-start
  433.8 8.6 collective-permute-start
  442.4 7.1 collective-permute-start
  449.6 6.9 collective-permute-start
  456.6 6.6 collective-permute-start
  463.3 7.4 collective-permute-start
  470.7 8.6 collective-permute-start
  479.5 7.5 collective-permute-start
  487.0 7.5 collective-permute-start
  494.6 8.2 collective-permute-start
  502.8 8.9 collective-permute-start
  511.9 9.2 collective-permute-start
  521.2 7.4 collective-permute-start
  529.3 384.4 %all-reduce.20.cloned.1.call-start = ((), (), s32[]{:S(2)}) async-start(), calls=%async_computation | async-start | bytes 262144 | tf_op jit(solution)/shard_map/psum | solution.py:193
  (45 other events, 872.6 us)
Sparse Core Ops, SparseCore 0:
  288.2 83.2 all-gather.4
  529.4 130.2 all-gather.6
  781.0 132.6 all-reduce.19
where the time goes:
time: 928 us; the launch traced here: 922 us
  waiting for transfers between devices  411 us (44%)
  starting transfers between devices  344 us (37%)
  blocking collectives  77.7 us (8%)
  other arithmetic  57.2 us (6%)
  between operations  15.1 us (2%)
  local copies, waits for them, and re-layouts  14.5 us (2%)
    ppermute x31, starting transfers between devices, shifted(): return lax.ppermute(value, axis, pairs)  161 us
    psum x1, waiting for transfers between devices, local(): grad_sum = lax.psum(grad_local, 'tm')  132 us
    ppermute x34, starting transfers between devices, with_halo(): before = lax.ppermute(last, axis, up)  127 us
    all_gather x2, waiting for transfers between devices, prefix(): pieces = jax.tree.map(lambda part: lax.all_gather(part, axis), value)  126 us
    psum x1, blocking collectives, local(): coef_sum = lax.psum(coef_local, ('tm', 'azi', 'rad'))  77.7 us
    ppermute x31, waiting for transfers between devices, shifted(): return lax.ppermute(value, axis, pairs)  75.1 us
    ppermute x34, waiting for transfers between devices, with_halo(): after = lax.ppermute(leading, axis, down)  65.4 us
    ppermute x34, starting transfers between devices, with_halo(): after = lax.ppermute(leading, axis, down)  56.4 us
  transfers between devices with their start and end apart: 102, of which 64 were waited for; matrix products, arithmetic and copies ran while one was open for 2% of the time, Pallas kernels for 0%

commit v1 on v0

v1 whole, which is shorter than its diff:
```python
import functools
import math

import jax
import jax.numpy as jnp
from jax import lax
from jax.experimental import pallas as pl
from jax.experimental.pallas import tpu as pltpu
from jax.sharding import PartitionSpec as P

STEPS = 2
SWEEPS = 8
DT_FINE = 0.25
LOWER_EDGE = 0.05
UPPER_EDGE = 1.95

BLOCKS = 8
RADS = 4
RB = 16
AB = 16
NZ = 128
ZB = NZ // BLOCKS
HALO = 2 * SWEEPS
WIN = ZB + 2 * HALO
SLICES = 32
GROUP = 2 * WIN
FIELDS = 4
ROWS = FIELDS * GROUP + 2 * ZB
PAD = 8
HALF = RB // 2
VMEM = 48 * 1024 * 1024


def lane_groups(tiles):
    tiles = list(tiles)
    lane = lax.broadcasted_iota(jnp.int32, tiles[0].shape, 1)
    for bit in (4, 2, 1):
        low = (lane & (16 * bit)) == 0
        for i in range(8):
            if i & bit:
                continue
            first, second = tiles[i], tiles[i + bit]
            tiles[i] = jnp.where(low, first, pltpu.roll(second, 16 * bit, 1))
            tiles[i + bit] = jnp.where(low, pltpu.roll(first, 128 - 16 * bit, 1), second)
    return tiles


def block_of(group):
    return (group % 2) * RADS + group // 2


def pack_kernel(start, target, cond, material, current, out):
    def turned(values):
        return jnp.transpose(values.reshape(HALF * AB, NZ))

    for half in range(2):
        own = pl.ds(half * HALF, HALF)
        mat = material[own]
        iron = jnp.where(mat == 1, 1.0, 0.0)
        source = jnp.where(mat == 2, current[own], 0.0)
        for field, values in enumerate((start[own], iron, cond[own], source)):
            flat = turned(values)
            padded = jnp.concatenate(
                [jnp.zeros((HALO, NZ), jnp.float32), flat, jnp.zeros((HALO, NZ), jnp.float32)], axis=0
            )
            for j in range(BLOCKS):
                out[pl.ds(j * ROWS + field * GROUP + half * WIN, WIN), :] = padded[ZB * j : ZB * j + WIN]
        flat = turned(target[own])
        for j in range(BLOCKS):
            out[pl.ds(j * ROWS + FIELDS * GROUP + half * ZB, ZB), :] = flat[ZB * j : ZB * (j + 1)]


def fine_kernel(coef, got, out, static, x, rho, iron, cond, source, sat, step_d, base, a_rp, a_rm, a_ap, a_am, a_zp, a_zm):
    b0, b1, b2 = coef[0], coef[1], coef[2]
    me = lax.axis_index("azi") * RADS + lax.axis_index("rad")
    slot = lax.axis_index("tm")

    def spread(field, dest, lift):
        for half in range(2):
            for tile in range(WIN // 8):
                rows = field * GROUP + half * WIN + tile * 8
                tiles = [got[pl.ds(block_of(g) * ROWS + rows, 8), :] for g in range(8)]
                for g, value in enumerate(lane_groups(tiles)):
                    dest(half * HALF + g, tile * 8, value)

    def to_x(i, row, value):
        x[0, i + 1, pl.ds(PAD + row, 8), :] = value

    def to(ref):
        def put(i, row, value):
            ref[i, pl.ds(row, 8), :] = value

        return put

    spread(0, to_x, PAD)
    spread(1, to(iron), 0)
    spread(2, to(cond), 0)
    spread(3, to(source), 0)

    blank = jnp.zeros((PAD, NZ), jnp.float32)
    for i in range(RB + 2):
        for buf in range(2):
            x[buf, i, pl.ds(0, PAD), :] = blank
            x[buf, i, pl.ds(PAD + WIN, PAD), :] = blank
        rho[i, pl.ds(0, PAD), :] = blank + 1.0
        rho[i, pl.ds(PAD + WIN, PAD), :] = blank + 1.0

    def wrap(ref_get, ref_put, size, outside):
        lane = lax.broadcasted_iota(jnp.int32, (size, NZ), 1)
        ref_put(0, jnp.where(lane < 32, outside, pltpu.roll(ref_get(RB), 32, 1)))
        ref_put(RB + 1, jnp.where(lane >= 96, outside, pltpu.roll(ref_get(1), 96, 1)))

    def wrap_x(buf, z0, nz):
        rows = pl.ds(PAD + z0, nz)

        def put(i, value):
            x[buf, i, rows, :] = value

        wrap(lambda i: x[buf, i, rows, :], put, nz, 0.0)

    def wrap_rho(z0, nz):
        rows = pl.ds(PAD + z0, nz)

        def put(i, value):
            rho[i, rows, :] = value

        wrap(lambda i: rho[i, rows, :], put, nz, 1.0)

    def prepare(buf, step, z0, nz):
        lane = lax.broadcasted_iota(jnp.int32, (nz, NZ), 1) & 31
        row = lax.broadcasted_iota(jnp.int32, (nz, NZ), 0) + (z0 - HALO) + me * ZB
        first, last = lane == 0, lane == 31
        rows = pl.ds(PAD + z0, nz)
        own = pl.ds(z0, nz)

        def curve(i, carry):
            u = x[buf, i + 1, rows, :]
            radial = 0.5 * (x[buf, i + 2, rows, :] - x[buf, i, rows, :])
            after = jnp.where(last, 0.0, pltpu.roll(u, NZ - 1, 1))
            before = jnp.where(first, 0.0, pltpu.roll(u, 1, 1))
            azimuthal = 0.5 * (after - before)
            square = radial * radial + azimuthal * azimuthal
            saturation = square / (1.0 + square)
            value = b2 + b0 * jnp.exp(b1 * saturation)
            rho[i + 1, rows, :] = jnp.where(iron[i, own, :] > 0.5, value, 1.0)
            if step == 0:
                sat[i] = saturation[HALO - z0 : HALO - z0 + ZB]
            return carry

        lax.fori_loop(0, RB, curve, 0)
        wrap_rho(z0, nz)
        angle = (4.0 * math.pi / (SLICES * STEPS)) * (slot * STEPS + (step + 1)).astype(jnp.float32)
        wave = jnp.cos(jnp.full((8, NZ), angle, jnp.float32))[0:1]

        def faces(i, carry):
            centre = rho[i + 1, rows, :]
            rp = 0.5 * (centre + rho[i + 2, rows, :])
            rm = 0.5 * (centre + rho[i, rows, :])
            ap = 0.5 * (centre + jnp.where(last, 1.0, pltpu.roll(centre, NZ - 1, 1)))
            am = 0.5 * (centre + jnp.where(first, 1.0, pltpu.roll(centre, 1, 1)))
            zp = 0.5 * (centre + rho[i + 1, pl.ds(PAD + z0 + 1, nz), :])
            zm = 0.5 * (centre + rho[i + 1, pl.ds(PAD + z0 - 1, nz), :])
            mass = cond[i, own, :] * (1.0 / DT_FINE)
            inverse = 1.0 / (mass + rp + rm + ap + am + zp + zm)
            a_rp[i, own, :] = inverse * rp
            a_rm[i, own, :] = inverse * rm
            a_ap[i, own, :] = jnp.where(last, 0.0, inverse * ap)
            a_am[i, own, :] = jnp.where(first, 0.0, inverse * am)
            a_zp[i, own, :] = jnp.where(row == NZ - 1, 0.0, inverse * zp)
            a_zm[i, own, :] = jnp.where(row == 0, 0.0, inverse * zm)
            base[i, own, :] = inverse * (mass * x[buf, i + 1, rows, :] + wave * source[i, own, :])
            return carry

        lax.fori_loop(0, RB, faces, 0)

    def sweep(buf, alpha, beta, z0, nz, wrapped):
        rows = pl.ds(PAD + z0, nz)
        own = pl.ds(z0, nz)

        def body(i, carry):
            centre = x[buf, i + 1, rows, :]
            total = base[i, own, :] - centre
            total = total + a_rp[i, own, :] * x[buf, i + 2, rows, :]
            total = total + a_rm[i, own, :] * x[buf, i, rows, :]
            total = total + a_ap[i, own, :] * pltpu.roll(centre, NZ - 1, 1)
            total = total + a_am[i, own, :] * pltpu.roll(centre, 1, 1)
            total = total + a_zp[i, own, :] * x[buf, i + 1, pl.ds(PAD + z0 + 1, nz), :]
            total = total + a_zm[i, own, :] * x[buf, i + 1, pl.ds(PAD + z0 - 1, nz), :]
            change = beta * total
            if alpha is not None:
                change = change + alpha * step_d[i, own, :]
            if wrapped:
                step_d[i, own, :] = change
            x[1 - buf, i + 1, rows, :] = centre + change
            return carry

        lax.fori_loop(0, RB, body, 0, unroll=2)

    theta = 0.5 * (UPPER_EDGE + LOWER_EDGE)
    delta = 0.5 * (UPPER_EDGE - LOWER_EDGE)
    scaled = theta / delta
    buf = 0
    wrap_x(0, 0, WIN)
    for step in range(STEPS):
        z0 = step * SWEEPS
        nz = WIN - 2 * z0
        prepare(buf, step, z0, nz)
        ratio = 1.0 / scaled
        alpha, beta = None, 1.0 / theta
        for index in range(SWEEPS):
            final = index == SWEEPS - 1
            if final:
                z0, nz = z0 + SWEEPS, nz - 2 * SWEEPS
            sweep(buf, alpha, beta, z0, nz, not final)
            buf = 1 - buf
            if not (final and step == STEPS - 1):
                wrap_x(buf, z0, nz)
            following = 1.0 / (2.0 * scaled - ratio)
            alpha, beta = following * ratio, 2.0 * following / delta
            ratio = following

    def put(kind, half, tile, block, value):
        out[pl.ds(((half * ZB + tile * 8) * 4 + kind) * 8 + block, 8, stride=32), :] = value

    for half in range(2):
        for tile in range(ZB // 8):
            ends = [x[buf, half * HALF + g + 1, pl.ds(PAD + HALO + tile * 8, 8), :] for g in range(8)]
            for g, value in enumerate(lane_groups(ends)):
                put(0, half, tile, block_of(g), value)
            sats = [sat[half * HALF + g, pl.ds(tile * 8, 8), :] for g in range(8)]
            for g, value in enumerate(lane_groups(sats)):
                put(1, half, tile, block_of(g), value)
            for block in range(BLOCKS):
                rows = block * ROWS + half * WIN + HALO + tile * 8
                put(2, half, tile, block, got[pl.ds(rows, 8), :])
                rows = block * ROWS + FIELDS * GROUP + half * ZB + tile * 8
                put(3, half, tile, block, got[pl.ds(rows, 8), :])

    place = (slot // ZB) * WIN + HALO + slot % ZB
    static[pl.ds(0, 8), :] = got[pl.ds(2 * GROUP + place, 8, stride=ROWS), :]
    static[pl.ds(8, 8), :] = got[pl.ds(1 * GROUP + place, 8, stride=ROWS), :]


def chain_kernel(coef, got, static, out, jumps, resids, factors, quads):
    b0, b1, b2 = coef[0], coef[1], coef[2]
    cond = static[pl.ds(0, 8), :]
    iron = static[pl.ds(8, 8), :]
    is_iron = iron > 0.5
    dt = STEPS * DT_FINE

    def part(n, kind):
        return got[pl.ds(n * 32 + kind * 8, 8), :]

    jump = jnp.zeros((8, NZ), jnp.float32)
    for n in range(SLICES):
        growth = jnp.exp(b1 * part(n, 1))
        lumped = 6.0 * jnp.where(is_iron, b2 + b0 * growth, 1.0)
        inverse = 1.0 / (cond + dt * lumped)
        factor = cond * inverse
        end = part(n, 0) + factor * jump
        out[pl.ds(n * 32, 8, stride=4), :] = end
        jumps[n] = jump
        resids[n] = end - part(n, 3)
        factors[n] = factor
        quads[n] = inverse * inverse
        if n < SLICES - 1:
            jump = end - part(n + 1, 2)

    tail = jnp.zeros((8, NZ), jnp.float32)
    grad = jnp.zeros((8, NZ), jnp.float32)
    sums = [jnp.zeros((8, NZ), jnp.float32) for _ in range(3)]
    for n in reversed(range(SLICES)):
        saturation = part(n, 1)
        growth = jnp.exp(b1 * saturation)
        lumped = 6.0 * jnp.where(is_iron, b2 + b0 * growth, 1.0)
        slope = resids[n] + tail
        scaled = slope * jumps[n] * quads[n]
        grad = grad + scaled * (dt * lumped)
        hterm = (6.0 * scaled) * (-dt * cond) * iron
        grown = hterm * growth
        sums[0] = sums[0] + grown
        sums[1] = sums[1] + grown * (b0 * saturation)
        sums[2] = sums[2] + hterm
        tail = factors[n] * slope
    lane = lax.broadcasted_iota(jnp.int32, (8, NZ), 1)
    totals = [jnp.sum(value, keepdims=True) for value in sums]
    row = jnp.where(lane == 0, totals[0], jnp.where(lane == 1, totals[1], jnp.where(lane == 2, totals[2], 0.0)))
    for n in range(SLICES):
        out[pl.ds(n * 32 + 1, 8, stride=4), :] = grad
        out[pl.ds(n * 32 + 2, 8, stride=4), :] = row
        out[pl.ds(n * 32 + 3, 8, stride=4), :] = row


def unpack_kernel(got, end, grad, coef_grad):
    for kind, dest in enumerate((end, grad)):
        for half in range(2):
            flat = jnp.concatenate(
                [got[pl.ds(half * ZB * 32 + j * 4 + kind, ZB, stride=32), :] for j in range(BLOCKS)], axis=0
            )
            dest[pl.ds(half * HALF, HALF)] = jnp.transpose(flat).reshape(HALF, AB, NZ)
    sums = jnp.sum(got[pl.ds(2, SLICES * BLOCKS, stride=4), :], axis=0, keepdims=True)
    lane = lax.broadcasted_iota(jnp.int32, (1, NZ), 1)
    count = SLICES * BLOCKS * RB * AB * NZ
    for c in range(3):
        coef_grad[c] = jnp.sum(jnp.where(lane == c, sums, 0.0)) * (1.0 / count)


def vmem():
    return pl.BlockSpec(memory_space=pltpu.VMEM)


def smem():
    return pl.BlockSpec(memory_space=pltpu.SMEM)


def call(kernel, outs, ins, scratch, out_specs=None):
    specs = [smem() if place == "s" else vmem() for place in ins]
    return pl.pallas_call(
        kernel,
        out_shape=outs,
        in_specs=specs,
        out_specs=out_specs if out_specs is not None else jax.tree.map(lambda leaf: vmem(), outs),
        scratch_shapes=scratch,
        compiler_params=pltpu.CompilerParams(vmem_limit_bytes=VMEM),
    )


def local(start_states, target, conductivity, material, current, bh_coef):
    def shape(*dims):
        return jax.ShapeDtypeStruct(dims, jnp.float32)

    packed = call(pack_kernel, shape(BLOCKS * ROWS, NZ), "vvvvv", [])(
        start_states[0], target[0], conductivity, material, current
    )
    whole = lax.all_to_all(packed, ("azi", "rad"), 0, 0, tiled=True)
    block = pltpu.VMEM((RB, WIN, NZ), jnp.float32)
    fine, static = call(
        fine_kernel,
        (shape(SLICES * 32, NZ), shape(16, NZ)),
        "sv",
        [
            pltpu.VMEM((2, RB + 2, WIN + 2 * PAD, NZ), jnp.float32),
            pltpu.VMEM((RB + 2, WIN + 2 * PAD, NZ), jnp.float32),
            block,
            block,
            block,
            pltpu.VMEM((RB, ZB, NZ), jnp.float32),
        ]
        + [block] * 8,
    )(bh_coef, whole)
    slices = lax.all_to_all(fine, "tm", 0, 0, tiled=True)
    line = pltpu.VMEM((SLICES, 8, NZ), jnp.float32)
    chained = call(chain_kernel, shape(SLICES * 32, NZ), "svv", [line] * 4)(bh_coef, slices, static)
    results = lax.all_to_all(chained, ("tm", "azi", "rad"), 0, 0, tiled=True)
    end, grad, coef_grad = call(
        unpack_kernel,
        (shape(RB, AB, NZ), shape(RB, AB, NZ), shape(3)),
        "v",
        [],
        out_specs=(vmem(), vmem(), smem()),
    )(results)
    return (end[None], grad, coef_grad)


def solution(mesh):
    placed = (
        P("tm", "rad", "azi", None),
        P("tm", "rad", "azi", None),
        P("rad", "azi", None),
        P("rad", "azi", None),
        P("rad", "azi", None),
        P(),
    )
    return jax.shard_map(
        local,
        mesh=mesh,
        in_specs=placed,
        out_specs=(P("tm", "rad", "azi", None), P("rad", "azi", None), P()),
        check_vma=False,
    )
```

time: 928 us -> 118 us (0.13)
  waiting for transfers between devices: 411 us -> 0 us
  starting transfers between devices: 344 us -> 0 us
  other arithmetic: 57.2 us -> 0 us
  Pallas kernels: 0 us -> 29.4 us
  between operations: 15.1 us -> 0.67 us
  local copies, waits for them, and re-layouts: 14.5 us -> 4.52 us
    ppermute x99 -> x0, starting transfers between devices: 344 us -> none  [the longest x31 161 us: shifted(): return lax.ppermute(value, axis, pairs)]
    ppermute x99 -> x0, waiting for transfers between devices: 153 us -> none  [the longest x31 75.1 us: shifted(): return lax.ppermute(value, axis, pairs)]
    psum x1 -> x0, waiting for transfers between devices: 132 us -> none  [local(): grad_sum = lax.psum(grad_local, 'tm')]
    all_gather x2 -> x0, waiting for transfers between devices: 126 us -> none  [prefix(): pieces = jax.tree.map(lambda part: lax.all_gather(part, axis), value)]
    all_to_all x0 -> x3, blocking collectives: none -> 83.5 us  [the longest x1 30.5 us: local(): results = lax.all_to_all(chained, ('tm', 'azi', 'rad'), 0, 0, tiled=True)]
    psum x1 -> x0, blocking collectives: 77.7 us -> none  [local(): coef_sum = lax.psum(coef_local, ('tm', 'azi', 'rad'))]
    select_n x64 -> x0, other arithmetic: 39.3 us -> none  [the longest x31 33.4 us: step(): jnp.where(position < mine, new, old)]
    pallas_call x0 -> x4, Pallas kernels: none -> 29.4 us  [the longest x1 27.4 us: local(): call(fine_kernel, (shape(SLICES * 32, NZ), shape(16, NZ)), 'sv', [pltpu.V...]
  transfers between devices with their start and end apart: 102 -> 0, of which waited for: 64 -> 0; matrix products, arithmetic and copies ran while one was open for 2% -> 0% of each run, Pallas kernels for 0% -> 0%
where the time goes in v1:
time: 118 us
  blocking collectives  83.5 us (71%)
  Pallas kernels  29.4 us (25%)
  local copies, waits for them, and re-layouts  4.52 us (4%)
    all_to_all x1, blocking collectives, local(): results = lax.all_to_all(chained, ('tm', 'azi', 'rad'), 0, 0, tiled=True)  30.5 us
    all_to_all x1, blocking collectives, local(): whole = lax.all_to_all(packed, ('azi', 'rad'), 0, 0, tiled=True)  28 us
    pallas_call x1, Pallas kernels, local(): call(fine_kernel, (shape(SLICES * 32, NZ), shape(16, NZ)), 'sv', [pltpu.V...  27.4 us
    all_to_all x1, blocking collectives, local(): slices = lax.all_to_all(fine, 'tm', 0, 0, tiled=True)  25 us
    unnamed x12, local copies, waits for them, and re-layouts  4.52 us

profile of v1, /device:TPU:1, one launch (start us, length us, event | category | flops | bytes accessed | tf_op | source)
XLA Modules:
  0.0 118.1 jit_solution(15264548780581921653)
XLA Ops:
  0.6 0.0 copy-start
  0.6 0.9 copy-done
  1.5 0.0 copy-start.1
  1.5 0.9 copy-done.1
  2.4 0.0 copy-start.2
  2.4 0.9 copy-done.2
  3.3 0.0 copy-start.3
  3.3 0.9 copy-done.3
  4.3 0.0 copy-start.4
  4.3 0.9 copy-done.4
  5.2 0.2 shard_map.85
  5.4 0.0 copy-start.5
  5.4 28.0 %all_to_all.33 = f32[8,416,128]{2,1,0:T(8,128)S(1)} all-to-all(f32[8,416,128]{2,1,0:T(8,128)S(1)} %bitcast.10), channel_id=1, replica_groups=mesh['tm'=32,'azi'=2,'rad'=4] {'azi','rad'}, dimensions={0} | all-to-all | bytes 3407872 | tf_op jit(solution)/shard_map/all_to_all | solution.py:335
  33.4 0.0 copy-done.5
  33.4 27.4 %shard_map.86 = (f32[1024,128]{1,0:T(8,128)S(1)}, f32[16,128]{1,0:T(8,128)S(1)}) custom-call(f32[3]{0:T(128)S(1)} %copy-done.5, f32[3328,128]{1,0:T(8,128)S(1)} %bitcast.9), custom_call_target="tpu_custom_call" | custom-call | tf_op jit(solution)/shard_map/pallas_call | solution.py:337
  60.8 25.0 %all_to_all.34 = f32[32,32,128]{2,1,0:T(8,128)S(1)} all-to-all(f32[32,32,128]{2,1,0:T(8,128)S(1)} %bitcast.14), channel_id=1, replica_groups=mesh['tm'=32,'azi'=2,'rad'=4] {'tm'}, dimensions={0} | all-to-all | bytes 1048576 | tf_op jit(solution)/shard_map/all_to_all | solution.py:351
  85.8 0.9 shard_map.87
  86.7 30.5 %all_to_all.35 = f32[256,4,128]{2,1,0:T(4,128)S(1)} all-to-all(f32[256,4,128]{2,1,0:T(4,128)S(1)} %bitcast.13), channel_id=1, replica_groups=mesh['tm'=32,'azi'=2,'rad'=4] {'tm','azi','rad'}, dimensions={0} | all-to-all | bytes 1048576 | tf_op jit(solution)/shard_map/all_to_all | solution.py:354
  117.2 0.9 shard_map.88
Async XLA Ops:
  0.6 0.9 copy-start
  1.5 0.9 copy-start.1
  2.4 0.9 copy-start.2
  3.3 0.9 copy-start.3
  4.3 0.9 copy-start.4
  5.4 28.0 %copy-start.5 = (f32[3]{0:T(128)S(1)}, f32[3]{0:T(128)}, u32[]{:S(2)}) copy-start(f32[3]{0:T(128)} %coef.3) | copy-start | bytes 40

commit v2 on v1

--- a/solution.py
+++ b/solution.py
@@ -49,28 +49,42 @@
     return (group % 2) * RADS + group // 2
 
 
-def pack_kernel(start, target, cond, material, current, out):
+def pack_kernel(start_at, target_at, cond_at, material_at, current_at, out, start, target, cond, material, current, sems):
+    pairs = ((start_at, start), (material_at, material), (cond_at, cond), (current_at, current), (target_at, target))
+    copies = [pltpu.make_async_copy(src, dst, sems.at[k]) for k, (src, dst) in enumerate(pairs)]
+    for copy in copies:
+        copy.start()
+
     def turned(values):
         return jnp.transpose(values.reshape(HALF * AB, NZ))
 
-    for half in range(2):
-        own = pl.ds(half * HALF, HALF)
-        mat = material[own]
-        iron = jnp.where(mat == 1, 1.0, 0.0)
-        source = jnp.where(mat == 2, current[own], 0.0)
-        for field, values in enumerate((start[own], iron, cond[own], source)):
-            flat = turned(values)
-            padded = jnp.concatenate(
-                [jnp.zeros((HALO, NZ), jnp.float32), flat, jnp.zeros((HALO, NZ), jnp.float32)], axis=0
-            )
-            for j in range(BLOCKS):
-                out[pl.ds(j * ROWS + field * GROUP + half * WIN, WIN), :] = padded[ZB * j : ZB * j + WIN]
-        flat = turned(target[own])
+    def put(field, half, values):
+        edge = jnp.zeros((HALO, NZ), jnp.float32)
+        padded = jnp.concatenate([edge, turned(values), edge], axis=0)
+        for j in range(BLOCKS):
+            out[pl.ds(j * ROWS + field * GROUP + half * WIN, WIN), :] = padded[ZB * j : ZB * j + WIN]
+
+    halves = [pl.ds(half * HALF, HALF) for half in range(2)]
+    copies[0].wait()
+    for half in range(2):
+        put(0, half, start[halves[half]])
+    copies[1].wait()
+    for half in range(2):
+        put(1, half, jnp.where(material[halves[half]] == 1, 1.0, 0.0))
+    copies[2].wait()
+    for half in range(2):
+        put(2, half, cond[halves[half]])
+    copies[3].wait()
+    for half in range(2):
+        put(3, half, jnp.where(material[halves[half]] == 2, current[halves[half]], 0.0))
+    copies[4].wait()
+    for half in range(2):
+        flat = turned(target[halves[half]])
         for j in range(BLOCKS):
             out[pl.ds(j * ROWS + FIELDS * GROUP + half * ZB, ZB), :] = flat[ZB * j : ZB * (j + 1)]
 
 
-def fine_kernel(coef, got, out, static, x, rho, iron, cond, source, sat, step_d, base, a_rp, a_rm, a_ap, a_am, a_zp, a_zm):
+def fine_kernel(coef, got, out, static, xa, xb, rho, iron, cond, source, sat, step_d, base, a_rp, a_rm, a_ap, a_am, a_zp, a_zm):
     b0, b1, b2 = coef[0], coef[1], coef[2]
     me = lax.axis_index("azi") * RADS + lax.axis_index("rad")
     slot = lax.axis_index("tm")
@@ -84,7 +98,7 @@
                     dest(half * HALF + g, tile * 8, value)
 
     def to_x(i, row, value):
-        x[0, i + 1, pl.ds(PAD + row, 8), :] = value
+        xa[i + 1, pl.ds(PAD + row, 8), :] = value
 
     def to(ref):
         def put(i, row, value):
@@ -92,16 +106,23 @@
 
         return put
 
-    spread(0, to_x, PAD)
-    spread(1, to(iron), 0)
-    spread(2, to(cond), 0)
-    spread(3, to(source), 0)
+    def some(tile, carry):
+        row = pl.multiple_of(tile * 8, 8)
+        for field, dest in ((0, to_x), (1, to(iron)), (2, to(cond)), (3, to(source))):
+            for half in range(2):
+                rows = field * GROUP + half * WIN + row
+                tiles = [got[pl.ds(pl.multiple_of(block_of(g) * ROWS + rows, 8), 8), :] for g in range(8)]
+                for g, value in enumerate(lane_groups(tiles)):
+                    dest(half * HALF + g, row, value)
+        return carry
+
+    lax.fori_loop(0, WIN // 8, some, 0)
 
     blank = jnp.zeros((PAD, NZ), jnp.float32)
     for i in range(RB + 2):
-        for buf in range(2):
-            x[buf, i, pl.ds(0, PAD), :] = blank
-            x[buf, i, pl.ds(PAD + WIN, PAD), :] = blank
+        for x in (xa, xb):
+            x[i, pl.ds(0, PAD), :] = blank
+            x[i, pl.ds(PAD + WIN, PAD), :] = blank
         rho[i, pl.ds(0, PAD), :] = blank + 1.0
         rho[i, pl.ds(PAD + WIN, PAD), :] = blank + 1.0
 
@@ -110,13 +131,13 @@
         ref_put(0, jnp.where(lane < 32, outside, pltpu.roll(ref_get(RB), 32, 1)))
         ref_put(RB + 1, jnp.where(lane >= 96, outside, pltpu.roll(ref_get(1), 96, 1)))
 
-    def wrap_x(buf, z0, nz):
+    def wrap_x(x, z0, nz):
         rows = pl.ds(PAD + z0, nz)
 
         def put(i, value):
-            x[buf, i, rows, :] = value
-
-        wrap(lambda i: x[buf, i, rows, :], put, nz, 0.0)
+            x[i, rows, :] = value
+
+        wrap(lambda i: x[i, rows, :], put, nz, 0.0)
 
     def wrap_rho(z0, nz):
         rows = pl.ds(PAD + z0, nz)
@@ -126,7 +147,7 @@
 
         wrap(lambda i: rho[i, rows, :], put, nz, 1.0)
 
-    def prepare(buf, step, z0, nz):
+    def prepare(x, step, z0, nz):
         lane = lax.broadcasted_iota(jnp.int32, (nz, NZ), 1) & 31
         row = lax.broadcasted_iota(jnp.int32, (nz, NZ), 0) + (z0 - HALO) + me * ZB
         first, last = lane == 0, lane == 31
@@ -134,8 +155,8 @@
         own = pl.ds(z0, nz)
 
         def curve(i, carry):
-            u = x[buf, i + 1, rows, :]
-            radial = 0.5 * (x[buf, i + 2, rows, :] - x[buf, i, rows, :])
+            u = x[i + 1, rows, :]
+            radial = 0.5 * (x[i + 2, rows, :] - x[i, rows, :])
             after = jnp.where(last, 0.0, pltpu.roll(u, NZ - 1, 1))
             before = jnp.where(first, 0.0, pltpu.roll(u, 1, 1))
             azimuthal = 0.5 * (after - before)
@@ -147,7 +168,8 @@
                 sat[i] = saturation[HALO - z0 : HALO - z0 + ZB]
             return carry
 
-        lax.fori_loop(0, RB, curve, 0)
+        for i in range(RB):
+            curve(i, 0)
         wrap_rho(z0, nz)
         angle = (4.0 * math.pi / (SLICES * STEPS)) * (slot * STEPS + (step + 1)).astype(jnp.float32)
         wave = jnp.cos(jnp.full((8, NZ), angle, jnp.float32))[0:1]
@@ -168,63 +190,74 @@
             a_am[i, own, :] = jnp.where(first, 0.0, inverse * am)
             a_zp[i, own, :] = jnp.where(row == NZ - 1, 0.0, inverse * zp)
             a_zm[i, own, :] = jnp.where(row == 0, 0.0, inverse * zm)
-            base[i, own, :] = inverse * (mass * x[buf, i + 1, rows, :] + wave * source[i, own, :])
+            base[i, own, :] = inverse * (mass * x[i + 1, rows, :] + wave * source[i, own, :])
             return carry
 
-        lax.fori_loop(0, RB, faces, 0)
-
-    def sweep(buf, alpha, beta, z0, nz, wrapped):
+        for i in range(RB):
+            faces(i, 0)
+
+    def sweep(x, fresh, alpha, beta, z0, nz, final):
         rows = pl.ds(PAD + z0, nz)
         own = pl.ds(z0, nz)
-
-        def body(i, carry):
-            centre = x[buf, i + 1, rows, :]
+        lane = lax.broadcasted_iota(jnp.int32, (nz, NZ), 1)
+        for i in range(RB):
+            centre = x[i + 1, rows, :]
             total = base[i, own, :] - centre
-            total = total + a_rp[i, own, :] * x[buf, i + 2, rows, :]
-            total = total + a_rm[i, own, :] * x[buf, i, rows, :]
+            total = total + a_rp[i, own, :] * x[i + 2, rows, :]
+            total = total + a_rm[i, own, :] * x[i, rows, :]
             total = total + a_ap[i, own, :] * pltpu.roll(centre, NZ - 1, 1)
             total = total + a_am[i, own, :] * pltpu.roll(centre, 1, 1)
-            total = total + a_zp[i, own, :] * x[buf, i + 1, pl.ds(PAD + z0 + 1, nz), :]
-            total = total + a_zm[i, own, :] * x[buf, i + 1, pl.ds(PAD + z0 - 1, nz), :]
+            total = total + a_zp[i, own, :] * x[i + 1, pl.ds(PAD + z0 + 1, nz), :]
+            total = total + a_zm[i, own, :] * x[i + 1, pl.ds(PAD + z0 - 1, nz), :]
             change = beta * total
             if alpha is not None:
                 change = change + alpha * step_d[i, own, :]
-            if wrapped:
+            if not final:
                 step_d[i, own, :] = change
-            x[1 - buf, i + 1, rows, :] = centre + change
-            return carry
-
-        lax.fori_loop(0, RB, body, 0, unroll=2)
+            value = centre + change
+            fresh[i + 1, rows, :] = value
+            if i == 0:
+                fresh[RB + 1, rows, :] = jnp.where(lane >= 96, 0.0, pltpu.roll(value, 96, 1))
+            if i == RB - 1:
+                fresh[0, rows, :] = jnp.where(lane < 32, 0.0, pltpu.roll(value, 32, 1))
 
     theta = 0.5 * (UPPER_EDGE + LOWER_EDGE)
     delta = 0.5 * (UPPER_EDGE - LOWER_EDGE)
     scaled = theta / delta
-    buf = 0
-    wrap_x(0, 0, WIN)
+    ratio, alphas, betas = 1.0 / scaled, [0.0], [1.0 / theta]
+    for index in range(SWEEPS - 1):
+        following = 1.0 / (2.0 * scaled - ratio)
+        alphas.append(following * ratio)
+        betas.append(2.0 * following / delta)
+        ratio = following
+
+    def pick(values, first, at):
+        chosen = jnp.float32(values[first])
+        for k in range(1, (SWEEPS - first) // 2):
+            chosen = jnp.where(at == k, jnp.float32(values[first + 2 * k]), chosen)
+        return chosen
+
+    wrap_x(xa, 0, WIN)
     for step in range(STEPS):
         z0 = step * SWEEPS
         nz = WIN - 2 * z0
-        prepare(buf, step, z0, nz)
-        ratio = 1.0 / scaled
-        alpha, beta = None, 1.0 / theta
-        for index in range(SWEEPS):
-            final = index == SWEEPS - 1
-            if final:
-                z0, nz = z0 + SWEEPS, nz - 2 * SWEEPS
-            sweep(buf, alpha, beta, z0, nz, not final)
-            buf = 1 - buf
-            if not (final and step == STEPS - 1):
-                wrap_x(buf, z0, nz)
-            following = 1.0 / (2.0 * scaled - ratio)
-            alpha, beta = following * ratio, 2.0 * following / delta
-            ratio = following
+        prepare(xa, step, z0, nz)
+        sweep(xa, xb, None, betas[0], z0, nz, False)
+
+        def pair(at, carry):
+            sweep(xb, xa, pick(alphas, 1, at), pick(betas, 1, at), z0, nz, False)
+            sweep(xa, xb, pick(alphas, 2, at), pick(betas, 2, at), z0, nz, False)
+            return carry
+
+        lax.fori_loop(0, (SWEEPS - 2) // 2, pair, 0)
+        sweep(xb, xa, alphas[-1], betas[-1], z0 + SWEEPS, nz - 2 * SWEEPS, True)
 
     def put(kind, half, tile, block, value):
         out[pl.ds(((half * ZB + tile * 8) * 4 + kind) * 8 + block, 8, stride=32), :] = value
 
     for half in range(2):
         for tile in range(ZB // 8):
-            ends = [x[buf, half * HALF + g + 1, pl.ds(PAD + HALO + tile * 8, 8), :] for g in range(8)]
+            ends = [xa[half * HALF + g + 1, pl.ds(PAD + HALO + tile * 8, 8), :] for g in range(8)]
             for g, value in enumerate(lane_groups(ends)):
                 put(0, half, tile, block_of(g), value)
             sats = [sat[half * HALF + g, pl.ds(tile * 8, 8), :] for g in range(8)]
@@ -258,7 +291,7 @@
         inverse = 1.0 / (cond + dt * lumped)
         factor = cond * inverse
         end = part(n, 0) + factor * jump
-        out[pl.ds(n * 32, 8, stride=4), :] = end
+        out[pl.ds(n * 24, 8, stride=3), :] = end
         jumps[n] = jump
         resids[n] = end - part(n, 3)
         factors[n] = factor
@@ -286,19 +319,18 @@
     totals = [jnp.sum(value, keepdims=True) for value in sums]
     row = jnp.where(lane == 0, totals[0], jnp.where(lane == 1, totals[1], jnp.where(lane == 2, totals[2], 0.0)))
     for n in range(SLICES):
-        out[pl.ds(n * 32 + 1, 8, stride=4), :] = grad
-        out[pl.ds(n * 32 + 2, 8, stride=4), :] = row
-        out[pl.ds(n * 32 + 3, 8, stride=4), :] = row
+        out[pl.ds(n * 24 + 1, 8, stride=3), :] = grad
+        out[pl.ds(n * 24 + 2, 8, stride=3), :] = row
 
 
 def unpack_kernel(got, end, grad, coef_grad):
     for kind, dest in enumerate((end, grad)):
         for half in range(2):
             flat = jnp.concatenate(
-                [got[pl.ds(half * ZB * 32 + j * 4 + kind, ZB, stride=32), :] for j in range(BLOCKS)], axis=0
+                [got[pl.ds(half * ZB * 24 + j * 3 + kind, ZB, stride=24), :] for j in range(BLOCKS)], axis=0
             )
             dest[pl.ds(half * HALF, HALF)] = jnp.transpose(flat).reshape(HALF, AB, NZ)
-    sums = jnp.sum(got[pl.ds(2, SLICES * BLOCKS, stride=4), :], axis=0, keepdims=True)
+    sums = jnp.sum(got[pl.ds(2, SLICES * BLOCKS, stride=3), :], axis=0, keepdims=True)
     lane = lax.broadcasted_iota(jnp.int32, (1, NZ), 1)
     count = SLICES * BLOCKS * RB * AB * NZ
     for c in range(3):
@@ -314,7 +346,8 @@
 
 
 def call(kernel, outs, ins, scratch, out_specs=None):
-    specs = [smem() if place == "s" else vmem() for place in ins]
+    spaces = {"s": pltpu.SMEM, "v": pltpu.VMEM, "a": pltpu.HBM}
+    specs = [pl.BlockSpec(memory_space=spaces[place]) for place in ins]
     return pl.pallas_call(
         kernel,
         out_shape=outs,
@@ -325,21 +358,19 @@
     )
 
 
-def local(start_states, target, conductivity, material, current, bh_coef):
-    def shape(*dims):
-        return jax.ShapeDtypeStruct(dims, jnp.float32)
-
-    packed = call(pack_kernel, shape(BLOCKS * ROWS, NZ), "vvvvv", [])(
-        start_states[0], target[0], conductivity, material, current
-    )
-    whole = lax.all_to_all(packed, ("azi", "rad"), 0, 0, tiled=True)
+def shape(*dims):
+    return jax.ShapeDtypeStruct(dims, jnp.float32)
+
+
+def solve(bh_coef, whole):
     block = pltpu.VMEM((RB, WIN, NZ), jnp.float32)
-    fine, static = call(
+    return call(
         fine_kernel,
         (shape(SLICES * 32, NZ), shape(16, NZ)),
         "sv",
         [
-            pltpu.VMEM((2, RB + 2, WIN + 2 * PAD, NZ), jnp.float32),
+            pltpu.VMEM((RB + 2, WIN + 2 * PAD, NZ), jnp.float32),
+            pltpu.VMEM((RB + 2, WIN + 2 * PAD, NZ), jnp.float32),
             pltpu.VMEM((RB + 2, WIN + 2 * PAD, NZ), jnp.float32),
             block,
             block,
@@ -348,10 +379,24 @@
         ]
         + [block] * 8,
     )(bh_coef, whole)
+
+
+def local(start_states, target, conductivity, material, current, bh_coef):
+    field = pltpu.VMEM((RB, AB, NZ), jnp.float32)
+    packed = call(
+        pack_kernel,
+        shape(BLOCKS * ROWS, NZ),
+        "aaaaa",
+        [field, field, field, pltpu.VMEM((RB, AB, NZ), jnp.int32), field, pltpu.SemaphoreType.DMA((5,))],
+    )(start_states[0], target[0], conductivity, material, current)
+    whole = lax.all_to_all(packed, ("azi", "rad"), 0, 0, tiled=True)
+    fine, static = solve(bh_coef, whole)
     slices = lax.all_to_all(fine, "tm", 0, 0, tiled=True)
     line = pltpu.VMEM((SLICES, 8, NZ), jnp.float32)
-    chained = call(chain_kernel, shape(SLICES * 32, NZ), "svv", [line] * 4)(bh_coef, slices, static)
-    results = lax.all_to_all(chained, ("tm", "azi", "rad"), 0, 0, tiled=True)
+    chained = call(chain_kernel, shape(SLICES * 24, NZ), "svv", [line] * 4)(bh_coef, slices, static)
+    results = lax.all_to_all(
+        chained.reshape(SLICES * BLOCKS, 1, 3 * NZ), ("tm", "azi", "rad"), 0, 0, tiled=True
+    ).reshape(SLICES * 24, NZ)
     end, grad, coef_grad = call(
         unpack_kernel,
         (shape(RB, AB, NZ), shape(RB, AB, NZ), shape(3)),

time: 118 us -> 99.5 us (0.84)
  Pallas kernels: 29.4 us -> 12.9 us
  blocking collectives: 83.5 us -> 81.2 us
    pallas_call x3, Pallas kernels: 28.5 us -> 12 us  [the longest x1 9.79 us: solve(): call(fine_kernel, (shape(SLICES * 32, NZ), shape(16, NZ)), 'sv', [pltpu.V...]
    all_to_all x1, blocking collectives: 30.5 us -> 28.2 us  [local(): lax.all_to_all(chained.reshape(SLICES * BLOCKS, 1, 3 * NZ), ('tm', 'azi',...]
where the time goes in v2:
time: 99.5 us; the launch traced here: 99.3 us
  blocking collectives  81.2 us (82%)
  Pallas kernels  12.9 us (13%)
  local copies, waits for them, and re-layouts  4.52 us (5%)
    all_to_all x1, blocking collectives, local(): lax.all_to_all(chained.reshape(SLICES * BLOCKS, 1, 3 * NZ), ('tm', 'azi',...  28.2 us
    all_to_all x1, blocking collectives, local(): whole = lax.all_to_all(packed, ('azi', 'rad'), 0, 0, tiled=True)  28 us
    all_to_all x1, blocking collectives, local(): slices = lax.all_to_all(fine, 'tm', 0, 0, tiled=True)  25 us
    pallas_call x1, Pallas kernels, solve(): call(fine_kernel, (shape(SLICES * 32, NZ), shape(16, NZ)), 'sv', [pltpu.V...  9.79 us
    unnamed x12, local copies, waits for them, and re-layouts  4.52 us

profile of v2, /device:TPU:1, one launch (start us, length us, event | category | flops | bytes accessed | tf_op | source)
XLA Modules:
  0.0 99.3 jit_solution(7300581403535866539)
XLA Ops:
  0.6 0.0 copy-start
  0.6 0.9 copy-done
  1.5 0.0 copy-start.1
  1.5 0.9 copy-done.1
  2.4 0.0 copy-start.2
  2.4 0.9 copy-done.2
  3.3 0.0 copy-start.3
  3.3 0.9 copy-done.3
  4.3 0.0 copy-start.4
  4.3 0.9 copy-done.4
  5.2 1.4 %shard_map.85 = f32[3328,128]{1,0:T(8,128)S(1)} custom-call(f32[16,16,128]{2,1,0:T(8,128)S(1)} %bitcast.15, f32[16,16,128]{2,1,0:T(8,128)S(1)} %bitcast.16, f32[16,16,128]{2,1,0:T(8,128)S(1)} %copy-done.2, s32[16,16,128]{2,1,0:T(8,128)S(1)} %copy-done.3, f32[16,16,128]{2,1,0:T(8,128)S(1)} %copy-done.4), custom_call_target="tpu_custom_call" | custom-call | tf_op jit(solution)/shard_map/pallas_call | solution.py:386
  6.5 0.0 copy-start.5
  6.5 28.0 %all_to_all.27 = f32[8,416,128]{2,1,0:T(8,128)S(1)} all-to-all(f32[8,416,128]{2,1,0:T(8,128)S(1)} %bitcast.10), channel_id=1, replica_groups=mesh['tm'=32,'azi'=2,'rad'=4] {'azi','rad'}, dimensions={0} | all-to-all | bytes 3407872 | tf_op jit(solution)/shard_map/all_to_all | solution.py:392
  34.5 0.0 copy-done.5
  34.5 9.8 %shard_map.86 = (f32[1024,128]{1,0:T(8,128)S(1)}, f32[16,128]{1,0:T(8,128)S(1)}) custom-call(f32[3]{0:T(128)S(1)} %copy-done.5, f32[3328,128]{1,0:T(8,128)S(1)} %bitcast.9), custom_call_target="tpu_custom_call" | custom-call | tf_op jit(solution)/shard_map/pallas_call | solution.py:367
  44.3 25.0 %all_to_all.28 = f32[32,32,128]{2,1,0:T(8,128)S(1)} all-to-all(f32[32,32,128]{2,1,0:T(8,128)S(1)} %bitcast.14), channel_id=1, replica_groups=mesh['tm'=32,'azi'=2,'rad'=4] {'tm'}, dimensions={0} | all-to-all | bytes 1048576 | tf_op jit(solution)/shard_map/all_to_all | solution.py:394
  69.3 0.9 shard_map.87
  70.2 28.2 %all_to_all.29 = f32[256,1,384]{2,1,0:T(1,128)S(1)} all-to-all(f32[256,1,384]{2,1,0:T(1,128)S(1)} %bitcast.13), channel_id=1, replica_groups=mesh['tm'=32,'azi'=2,'rad'=4] {'tm','azi','rad'}, dimensions={0} | all-to-all | bytes 786432 | tf_op jit(solution)/shard_map/all_to_all | solution.py:397
  98.4 0.9 shard_map.88
Async XLA Ops:
  0.6 0.9 copy-start
  1.5 0.9 copy-start.1
  2.4 0.9 copy-start.2
  3.3 0.9 copy-start.3
  4.3 0.9 copy-start.4
  6.5 28.0 %copy-start.5 = (f32[3]{0:T(128)S(1)}, f32[3]{0:T(128)}, u32[]{:S(2)}) copy-start(f32[3]{0:T(128)} %coef.3) | copy-start | bytes 40

commit v3 on v2

--- a/solution.py
+++ b/solution.py
@@ -29,6 +29,7 @@
 PAD = 8
 HALF = RB // 2
 VMEM = 48 * 1024 * 1024
+WHOLE_VMEM = 56 * 1024 * 1024
 
 
 def lane_groups(tiles):
@@ -346,7 +347,7 @@
 
 
 def call(kernel, outs, ins, scratch, out_specs=None):
-    spaces = {"s": pltpu.SMEM, "v": pltpu.VMEM, "a": pltpu.HBM}
+    spaces = {"s": pltpu.SMEM, "v": pltpu.VMEM, "h": pltpu.HBM}
     specs = [pl.BlockSpec(memory_space=spaces[place]) for place in ins]
     return pl.pallas_call(
         kernel,
@@ -354,7 +355,7 @@
         in_specs=specs,
         out_specs=out_specs if out_specs is not None else jax.tree.map(lambda leaf: vmem(), outs),
         scratch_shapes=scratch,
-        compiler_params=pltpu.CompilerParams(vmem_limit_bytes=VMEM),
+        compiler_params=pltpu.CompilerParams(vmem_limit_bytes=WHOLE_VMEM if "h" in ins else VMEM),
     )
 
 
@@ -386,7 +387,7 @@
     packed = call(
         pack_kernel,
         shape(BLOCKS * ROWS, NZ),
-        "aaaaa",
+        "hhhhh",
         [field, field, field, pltpu.VMEM((RB, AB, NZ), jnp.int32), field, pltpu.SemaphoreType.DMA((5,))],
     )(start_states[0], target[0], conductivity, material, current)
     whole = lax.all_to_all(packed, ("azi", "rad"), 0, 0, tiled=True)

time: 99.5 us -> 96.5 us (0.970)
  local copies, waits for them, and re-layouts: 4.52 us -> 0.01 us
  Pallas kernels: 12.9 us -> 14.2 us
    unnamed x12 -> x2, local copies, waits for them, and re-layouts: 4.52 us -> 0.01 us
    pallas_call x1, Pallas kernels: 1.36 us -> 2.65 us  [local(): call(pack_kernel, shape(BLOCKS * ROWS, NZ), 'hhhhh', [field, field, field...]
    all_to_all x1, blocking collectives: 28 us -> 29.1 us  [local(): whole = lax.all_to_all(packed, ('azi', 'rad'), 0, 0, tiled=True)]
where the time goes in v3:
time: 96.5 us; the launch traced here: 96.2 us
  blocking collectives  81.4 us (84%)
  Pallas kernels  14.2 us (15%)
    all_to_all x1, blocking collectives, local(): whole = lax.all_to_all(packed, ('azi', 'rad'), 0, 0, tiled=True)  29.1 us
    all_to_all x1, blocking collectives, local(): lax.all_to_all(chained.reshape(SLICES * BLOCKS, 1, 3 * NZ), ('tm', 'azi',...  28.2 us
    all_to_all x1, blocking collectives, local(): slices = lax.all_to_all(fine, 'tm', 0, 0, tiled=True)  24.1 us
    pallas_call x1, Pallas kernels, solve(): call(fine_kernel, (shape(SLICES * 32, NZ), shape(16, NZ)), 'sv', [pltpu.V...  9.79 us
    pallas_call x1, Pallas kernels, local(): call(pack_kernel, shape(BLOCKS * ROWS, NZ), 'hhhhh', [field, field, field...  2.65 us

profile of v3, /device:TPU:1, one launch (start us, length us, event | category | flops | bytes accessed | tf_op | source)
XLA Modules:
  0.0 96.2 jit_solution(10473829139899853801)
XLA Ops:
  0.6 2.7 %shard_map.85 = f32[3328,128]{1,0:T(8,128)} custom-call(f32[16,16,128]{2,1,0:T(8,128)} %bitcast.15, f32[16,16,128]{2,1,0:T(8,128)} %bitcast.16, f32[16,16,128]{2,1,0:T(8,128)} %cond_at.1, s32[16,16,128]{2,1,0:T(8,128)} %material_at.1, f32[16,16,128]{2,1,0:T(8,128)} %current_at.1), custom_call_target="tpu_custom_call" | custom-call | tf_op jit(solution)/shard_map/pallas_call | solution.py:387
  3.3 0.0 copy-start
  3.3 29.1 %all_to_all.27 = f32[8,416,128]{2,1,0:T(8,128)S(1)} all-to-all(f32[8,416,128]{2,1,0:T(8,128)} %bitcast.14), channel_id=1, replica_groups=mesh['tm'=32,'azi'=2,'rad'=4] {'azi','rad'}, dimensions={0} | all-to-all | bytes 3407872 | tf_op jit(solution)/shard_map/all_to_all | solution.py:393
  32.4 0.0 copy-done
  32.4 9.8 %shard_map.86 = (f32[1024,128]{1,0:T(8,128)S(1)}, f32[16,128]{1,0:T(8,128)S(1)}) custom-call(f32[3]{0:T(128)S(1)} %copy-done, f32[3328,128]{1,0:T(8,128)S(1)} %bitcast.9), custom_call_target="tpu_custom_call" | custom-call | tf_op jit(solution)/shard_map/pallas_call | solution.py:368
  42.2 24.1 %all_to_all.28 = f32[32,32,128]{2,1,0:T(8,128)S(1)} all-to-all(f32[32,32,128]{2,1,0:T(8,128)S(1)} %bitcast.13), channel_id=1, replica_groups=mesh['tm'=32,'azi'=2,'rad'=4] {'tm'}, dimensions={0} | all-to-all | bytes 1048576 | tf_op jit(solution)/shard_map/all_to_all | solution.py:395
  66.3 0.9 shard_map.87
  67.2 28.2 %all_to_all.29 = f32[256,1,384]{2,1,0:T(1,128)S(1)} all-to-all(f32[256,1,384]{2,1,0:T(1,128)S(1)} %bitcast.12), channel_id=1, replica_groups=mesh['tm'=32,'azi'=2,'rad'=4] {'tm','azi','rad'}, dimensions={0} | all-to-all | bytes 786432 | tf_op jit(solution)/shard_map/all_to_all | solution.py:398
  95.4 0.9 shard_map.88
Async XLA Ops:
  3.3 29.1 %copy-start = (f32[3]{0:T(128)S(1)}, f32[3]{0:T(128)}, u32[]{:S(2)}) copy-start(f32[3]{0:T(128)} %coef.3) | copy-start | bytes 40

commit v4 on v3

--- a/solution.py
+++ b/solution.py
@@ -27,22 +27,34 @@
 FIELDS = 4
 ROWS = FIELDS * GROUP + 2 * ZB
 PAD = 8
-HALF = RB // 2
 VMEM = 48 * 1024 * 1024
 WHOLE_VMEM = 56 * 1024 * 1024
+
+
+STRIDES = ((4, 64), (2, 32), (1, 8))
+INNER = 8
+
+
+def rows_of(half):
+    for t in range(16):
+        yield ((t >> 1) & 1) * 8 + half * 4 + ((t >> 3) & 1) * 2 + ((t >> 2) & 1), t & 1
 
 
 def lane_groups(tiles):
     tiles = list(tiles)
     lane = lax.broadcasted_iota(jnp.int32, tiles[0].shape, 1)
-    for bit in (4, 2, 1):
-        low = (lane & (16 * bit)) == 0
+    for bit, stride in STRIDES:
+        low = (lane & stride) == 0
         for i in range(8):
             if i & bit:
                 continue
             first, second = tiles[i], tiles[i + bit]
-            tiles[i] = jnp.where(low, first, pltpu.roll(second, 16 * bit, 1))
-            tiles[i + bit] = jnp.where(low, pltpu.roll(first, 128 - 16 * bit, 1), second)
+            if 2 * stride == NZ:
+                moved = pltpu.roll(jnp.where(low, second, first), stride, 1)
+                tiles[i], tiles[i + bit] = jnp.where(low, first, moved), jnp.where(low, moved, second)
+            else:
+                tiles[i] = jnp.where(low, first, pltpu.roll(second, stride, 1))
+                tiles[i + bit] = jnp.where(low, pltpu.roll(first, NZ - stride, 1), second)
     return tiles
 
 
@@ -56,31 +68,30 @@
     for copy in copies:
         copy.start()
 
-    def turned(values):
-        return jnp.transpose(values.reshape(HALF * AB, NZ))
-
-    def put(field, half, values):
+    def turned(read, half):
+        return jnp.transpose(jnp.concatenate([read(r, pl.ds(q, 8, stride=2)) for r, q in rows_of(half)], axis=0))
+
+    def put(field, half, read):
         edge = jnp.zeros((HALO, NZ), jnp.float32)
-        padded = jnp.concatenate([edge, turned(values), edge], axis=0)
+        padded = jnp.concatenate([edge, turned(read, half), edge], axis=0)
         for j in range(BLOCKS):
             out[pl.ds(j * ROWS + field * GROUP + half * WIN, WIN), :] = padded[ZB * j : ZB * j + WIN]
 
-    halves = [pl.ds(half * HALF, HALF) for half in range(2)]
     copies[0].wait()
     for half in range(2):
-        put(0, half, start[halves[half]])
+        put(0, half, lambda r, q: start[r, q, :])
     copies[1].wait()
     for half in range(2):
-        put(1, half, jnp.where(material[halves[half]] == 1, 1.0, 0.0))
+        put(1, half, lambda r, q: jnp.where(material[r, q, :] == 1, 1.0, 0.0))
     copies[2].wait()
     for half in range(2):
-        put(2, half, cond[halves[half]])
+        put(2, half, lambda r, q: cond[r, q, :])
     copies[3].wait()
     for half in range(2):
-        put(3, half, jnp.where(material[halves[half]] == 2, current[halves[half]], 0.0))
+        put(3, half, lambda r, q: jnp.where(material[r, q, :] == 2, current[r, q, :], 0.0))
     copies[4].wait()
     for half in range(2):
-        flat = turned(target[halves[half]])
+        flat = turned(lambda r, q: target[r, q, :], half)
         for j in range(BLOCKS):
             out[pl.ds(j * ROWS + FIELDS * GROUP + half * ZB, ZB), :] = flat[ZB * j : ZB * (j + 1)]
 
@@ -90,20 +101,15 @@
     me = lax.axis_index("azi") * RADS + lax.axis_index("rad")
     slot = lax.axis_index("tm")
 
-    def spread(field, dest, lift):
-        for half in range(2):
-            for tile in range(WIN // 8):
-                rows = field * GROUP + half * WIN + tile * 8
-                tiles = [got[pl.ds(block_of(g) * ROWS + rows, 8), :] for g in range(8)]
-                for g, value in enumerate(lane_groups(tiles)):
-                    dest(half * HALF + g, tile * 8, value)
-
-    def to_x(i, row, value):
-        xa[i + 1, pl.ds(PAD + row, 8), :] = value
+    def edged(q, s):
+        return q * (INNER + 2) + s + 1
+
+    def to_x(q, s, row, value):
+        xa[edged(q, s), pl.ds(PAD + row, 8), :] = value
 
     def to(ref):
-        def put(i, row, value):
-            ref[i, pl.ds(row, 8), :] = value
+        def put(q, s, row, value):
+            ref[q * INNER + s, pl.ds(row, 8), :] = value
 
         return put
 
@@ -114,23 +120,26 @@
                 rows = field * GROUP + half * WIN + row
                 tiles = [got[pl.ds(pl.multiple_of(block_of(g) * ROWS + rows, 8), 8), :] for g in range(8)]
                 for g, value in enumerate(lane_groups(tiles)):
-                    dest(half * HALF + g, row, value)
+                    dest(g & 1, half * 4 + (g >> 1), row, value)
         return carry
 
     lax.fori_loop(0, WIN // 8, some, 0)
 
     blank = jnp.zeros((PAD, NZ), jnp.float32)
-    for i in range(RB + 2):
+    for i in range(2 * (INNER + 2)):
         for x in (xa, xb):
             x[i, pl.ds(0, PAD), :] = blank
             x[i, pl.ds(PAD + WIN, PAD), :] = blank
         rho[i, pl.ds(0, PAD), :] = blank + 1.0
         rho[i, pl.ds(PAD + WIN, PAD), :] = blank + 1.0
 
-    def wrap(ref_get, ref_put, size, outside):
+    def wrap(get, put, size, outside):
         lane = lax.broadcasted_iota(jnp.int32, (size, NZ), 1)
-        ref_put(0, jnp.where(lane < 32, outside, pltpu.roll(ref_get(RB), 32, 1)))
-        ref_put(RB + 1, jnp.where(lane >= 96, outside, pltpu.roll(ref_get(1), 96, 1)))
+        for q in range(2):
+            last = pltpu.roll(get(edged(q, INNER - 1)), 16, 1)
+            put(edged(q, -1), jnp.where(lane < 16, outside, last))
+            first = pltpu.roll(get(edged(q, 0)), NZ - 16, 1)
+            put(edged(q, INNER), jnp.where(lane >= NZ - 16, outside, first))
 
     def wrap_x(x, z0, nz):
         rows = pl.ds(PAD + z0, nz)
@@ -149,78 +158,86 @@
         wrap(lambda i: rho[i, rows, :], put, nz, 1.0)
 
     def prepare(x, step, z0, nz):
-        lane = lax.broadcasted_iota(jnp.int32, (nz, NZ), 1) & 31
+        lane = lax.broadcasted_iota(jnp.int32, (nz, NZ), 1) & 15
         row = lax.broadcasted_iota(jnp.int32, (nz, NZ), 0) + (z0 - HALO) + me * ZB
-        first, last = lane == 0, lane == 31
         rows = pl.ds(PAD + z0, nz)
         own = pl.ds(z0, nz)
 
-        def curve(i, carry):
-            u = x[i + 1, rows, :]
-            radial = 0.5 * (x[i + 2, rows, :] - x[i, rows, :])
-            after = jnp.where(last, 0.0, pltpu.roll(u, NZ - 1, 1))
-            before = jnp.where(first, 0.0, pltpu.roll(u, 1, 1))
-            azimuthal = 0.5 * (after - before)
-            square = radial * radial + azimuthal * azimuthal
-            saturation = square / (1.0 + square)
-            value = b2 + b0 * jnp.exp(b1 * saturation)
-            rho[i + 1, rows, :] = jnp.where(iron[i, own, :] > 0.5, value, 1.0)
-            if step == 0:
-                sat[i] = saturation[HALO - z0 : HALO - z0 + ZB]
-            return carry
-
-        for i in range(RB):
-            curve(i, 0)
+        def azimuths(ref, q, s, outside):
+            beside = ref[edged(1 - q, s), rows, :]
+            if q == 0:
+                return beside, jnp.where(lane == 0, outside, pltpu.roll(beside, 1, 1))
+            return jnp.where(lane == 15, outside, pltpu.roll(beside, NZ - 1, 1)), beside
+
+        for q in range(2):
+            for s in range(INNER):
+                i, at = q * INNER + s, edged(q, s)
+                radial = 0.5 * (x[at + 1, rows, :] - x[at - 1, rows, :])
+                up, down = azimuths(x, q, s, 0.0)
+                azimuthal = 0.5 * (up - down)
+                square = radial * radial + azimuthal * azimuthal
+                saturation = square / (1.0 + square)
+                value = b2 + b0 * jnp.exp(b1 * saturation)
+                rho[at, rows, :] = jnp.where(iron[i, own, :] > 0.5, value, 1.0)
+                if step == 0:
+                    sat[i] = saturation[HALO - z0 : HALO - z0 + ZB]
+
         wrap_rho(z0, nz)
         angle = (4.0 * math.pi / (SLICES * STEPS)) * (slot * STEPS + (step + 1)).astype(jnp.float32)
         wave = jnp.cos(jnp.full((8, NZ), angle, jnp.float32))[0:1]
 
-        def faces(i, carry):
-            centre = rho[i + 1, rows, :]
-            rp = 0.5 * (centre + rho[i + 2, rows, :])
-            rm = 0.5 * (centre + rho[i, rows, :])
-            ap = 0.5 * (centre + jnp.where(last, 1.0, pltpu.roll(centre, NZ - 1, 1)))
-            am = 0.5 * (centre + jnp.where(first, 1.0, pltpu.roll(centre, 1, 1)))
-            zp = 0.5 * (centre + rho[i + 1, pl.ds(PAD + z0 + 1, nz), :])
-            zm = 0.5 * (centre + rho[i + 1, pl.ds(PAD + z0 - 1, nz), :])
-            mass = cond[i, own, :] * (1.0 / DT_FINE)
-            inverse = 1.0 / (mass + rp + rm + ap + am + zp + zm)
-            a_rp[i, own, :] = inverse * rp
-            a_rm[i, own, :] = inverse * rm
-            a_ap[i, own, :] = jnp.where(last, 0.0, inverse * ap)
-            a_am[i, own, :] = jnp.where(first, 0.0, inverse * am)
-            a_zp[i, own, :] = jnp.where(row == NZ - 1, 0.0, inverse * zp)
-            a_zm[i, own, :] = jnp.where(row == 0, 0.0, inverse * zm)
-            base[i, own, :] = inverse * (mass * x[i + 1, rows, :] + wave * source[i, own, :])
-            return carry
-
-        for i in range(RB):
-            faces(i, 0)
+        for q in range(2):
+            for s in range(INNER):
+                i, at = q * INNER + s, edged(q, s)
+                centre = rho[at, rows, :]
+                up, down = azimuths(rho, q, s, 1.0)
+                rp = 0.5 * (centre + rho[at + 1, rows, :])
+                rm = 0.5 * (centre + rho[at - 1, rows, :])
+                ap = 0.5 * (centre + up)
+                am = 0.5 * (centre + down)
+                zp = 0.5 * (centre + rho[at, pl.ds(PAD + z0 + 1, nz), :])
+                zm = 0.5 * (centre + rho[at, pl.ds(PAD + z0 - 1, nz), :])
+                mass = cond[i, own, :] * (1.0 / DT_FINE)
+                inverse = 1.0 / (mass + rp + rm + ap + am + zp + zm)
+                a_rp[i, own, :] = inverse * rp
+                a_rm[i, own, :] = inverse * rm
+                a_ap[i, own, :] = jnp.where(lane == 15, 0.0, inverse * ap) if q else inverse * ap
+                a_am[i, own, :] = inverse * am if q else jnp.where(lane == 0, 0.0, inverse * am)
+                a_zp[i, own, :] = jnp.where(row == NZ - 1, 0.0, inverse * zp)
+                a_zm[i, own, :] = jnp.where(row == 0, 0.0, inverse * zm)
+                base[i, own, :] = inverse * (mass * x[at, rows, :] + wave * source[i, own, :])
 
     def sweep(x, fresh, alpha, beta, z0, nz, final):
         rows = pl.ds(PAD + z0, nz)
         own = pl.ds(z0, nz)
         lane = lax.broadcasted_iota(jnp.int32, (nz, NZ), 1)
-        for i in range(RB):
-            centre = x[i + 1, rows, :]
-            total = base[i, own, :] - centre
-            total = total + a_rp[i, own, :] * x[i + 2, rows, :]
-            total = total + a_rm[i, own, :] * x[i, rows, :]
-            total = total + a_ap[i, own, :] * pltpu.roll(centre, NZ - 1, 1)
-            total = total + a_am[i, own, :] * pltpu.roll(centre, 1, 1)
-            total = total + a_zp[i, own, :] * x[i + 1, pl.ds(PAD + z0 + 1, nz), :]
-            total = total + a_zm[i, own, :] * x[i + 1, pl.ds(PAD + z0 - 1, nz), :]
-            change = beta * total
-            if alpha is not None:
-                change = change + alpha * step_d[i, own, :]
-            if not final:
-                step_d[i, own, :] = change
-            value = centre + change
-            fresh[i + 1, rows, :] = value
-            if i == 0:
-                fresh[RB + 1, rows, :] = jnp.where(lane >= 96, 0.0, pltpu.roll(value, 96, 1))
-            if i == RB - 1:
-                fresh[0, rows, :] = jnp.where(lane < 32, 0.0, pltpu.roll(value, 32, 1))
+        for s in range(INNER):
+            for q in range(2):
+                i, at = q * INNER + s, edged(q, s)
+                centre = x[at, rows, :]
+                beside = x[edged(1 - q, s), rows, :]
+                rolled = pltpu.roll(beside, NZ - 1 if q else 1, 1)
+                up, down = (rolled, beside) if q else (beside, rolled)
+                total = base[i, own, :] - centre
+                total = total + a_rp[i, own, :] * x[at + 1, rows, :]
+                total = total + a_rm[i, own, :] * x[at - 1, rows, :]
+                total = total + a_ap[i, own, :] * up
+                total = total + a_am[i, own, :] * down
+                total = total + a_zp[i, own, :] * x[at, pl.ds(PAD + z0 + 1, nz), :]
+                total = total + a_zm[i, own, :] * x[at, pl.ds(PAD + z0 - 1, nz), :]
+                change = beta * total
+                if alpha is not None:
+                    change = change + alpha * step_d[i, own, :]
+                if not final:
+                    step_d[i, own, :] = change
+                value = centre + change
+                fresh[at, rows, :] = value
+                if s == 0:
+                    first = pltpu.roll(value, NZ - 16, 1)
+                    fresh[edged(q, INNER), rows, :] = jnp.where(lane >= NZ - 16, 0.0, first)
+                if s == INNER - 1:
+                    last = pltpu.roll(value, 16, 1)
+                    fresh[edged(q, -1), rows, :] = jnp.where(lane < 16, 0.0, last)
 
     theta = 0.5 * (UPPER_EDGE + LOWER_EDGE)
     delta = 0.5 * (UPPER_EDGE - LOWER_EDGE)
@@ -258,10 +275,10 @@
 
     for half in range(2):
         for tile in range(ZB // 8):
-            ends = [xa[half * HALF + g + 1, pl.ds(PAD + HALO + tile * 8, 8), :] for g in range(8)]
+            ends = [xa[edged(g & 1, half * 4 + (g >> 1)), pl.ds(PAD + HALO + tile * 8, 8), :] for g in range(8)]
             for g, value in enumerate(lane_groups(ends)):
                 put(0, half, tile, block_of(g), value)
-            sats = [sat[half * HALF + g, pl.ds(tile * 8, 8), :] for g in range(8)]
+            sats = [sat[(g & 1) * INNER + half * 4 + (g >> 1), pl.ds(tile * 8, 8), :] for g in range(8)]
             for g, value in enumerate(lane_groups(sats)):
                 put(1, half, tile, block_of(g), value)
             for block in range(BLOCKS):
@@ -330,7 +347,9 @@
             flat = jnp.concatenate(
                 [got[pl.ds(half * ZB * 24 + j * 3 + kind, ZB, stride=24), :] for j in range(BLOCKS)], axis=0
             )
-            dest[pl.ds(half * HALF, HALF)] = jnp.transpose(flat).reshape(HALF, AB, NZ)
+            turned = jnp.transpose(flat)
+            for t, (r, q) in enumerate(rows_of(half)):
+                dest[r, pl.ds(q, 8, stride=2), :] = turned[8 * t : 8 * t + 8]
     sums = jnp.sum(got[pl.ds(2, SLICES * BLOCKS, stride=3), :], axis=0, keepdims=True)
     lane = lax.broadcasted_iota(jnp.int32, (1, NZ), 1)
     count = SLICES * BLOCKS * RB * AB * NZ
@@ -370,9 +389,9 @@
         (shape(SLICES * 32, NZ), shape(16, NZ)),
         "sv",
         [
-            pltpu.VMEM((RB + 2, WIN + 2 * PAD, NZ), jnp.float32),
-            pltpu.VMEM((RB + 2, WIN + 2 * PAD, NZ), jnp.float32),
-            pltpu.VMEM((RB + 2, WIN + 2 * PAD, NZ), jnp.float32),
+            pltpu.VMEM((2 * (INNER + 2), WIN + 2 * PAD, NZ), jnp.float32),
+            pltpu.VMEM((2 * (INNER + 2), WIN + 2 * PAD, NZ), jnp.float32),
+            pltpu.VMEM((2 * (INNER + 2), WIN + 2 * PAD, NZ), jnp.float32),
             block,
             block,
             block,

time: 96.5 us -> 95.3 us (0.988)
  Pallas kernels: 14.2 us -> 13 us
    pallas_call x1, Pallas kernels: 9.79 us -> 8.6 us  [solve(): call(fine_kernel, (shape(SLICES * 32, NZ), shape(16, NZ)), 'sv', [pltpu.V...]
where the time goes in v4:
time: 95.3 us; the launch traced here: 95.1 us
  blocking collectives  81.4 us (85%)
  Pallas kernels  13 us (14%)
    all_to_all x1, blocking collectives, local(): whole = lax.all_to_all(packed, ('azi', 'rad'), 0, 0, tiled=True)  29.1 us
    all_to_all x1, blocking collectives, local(): lax.all_to_all(chained.reshape(SLICES * BLOCKS, 1, 3 * NZ), ('tm', 'azi',...  28.2 us
    all_to_all x1, blocking collectives, local(): slices = lax.all_to_all(fine, 'tm', 0, 0, tiled=True)  24.1 us
    pallas_call x1, Pallas kernels, solve(): call(fine_kernel, (shape(SLICES * 32, NZ), shape(16, NZ)), 'sv', [pltpu.V...  8.6 us
    pallas_call x1, Pallas kernels, local(): call(pack_kernel, shape(BLOCKS * ROWS, NZ), 'hhhhh', [field, field, field...  2.65 us

profile of v4, /device:TPU:1, one launch (start us, length us, event | category | flops | bytes accessed | tf_op | source)
XLA Modules:
  0.0 95.1 jit_solution(2907593017362033967)
XLA Ops:
  0.6 2.7 %shard_map.85 = f32[3328,128]{1,0:T(8,128)} custom-call(f32[16,16,128]{2,1,0:T(8,128)} %bitcast.15, f32[16,16,128]{2,1,0:T(8,128)} %bitcast.16, f32[16,16,128]{2,1,0:T(8,128)} %cond_at.1, s32[16,16,128]{2,1,0:T(8,128)} %material_at.1, f32[16,16,128]{2,1,0:T(8,128)} %current_at.1), custom_call_target="tpu_custom_call" | custom-call | tf_op jit(solution)/shard_map/pallas_call | solution.py:406
  3.3 0.0 copy-start
  3.3 29.1 %all_to_all.27 = f32[8,416,128]{2,1,0:T(8,128)S(1)} all-to-all(f32[8,416,128]{2,1,0:T(8,128)} %bitcast.14), channel_id=1, replica_groups=mesh['tm'=32,'azi'=2,'rad'=4] {'azi','rad'}, dimensions={0} | all-to-all | bytes 3407872 | tf_op jit(solution)/shard_map/all_to_all | solution.py:412
  32.4 0.0 copy-done
  32.4 8.6 %shard_map.86 = (f32[1024,128]{1,0:T(8,128)S(1)}, f32[16,128]{1,0:T(8,128)S(1)}) custom-call(f32[3]{0:T(128)S(1)} %copy-done, f32[3328,128]{1,0:T(8,128)S(1)} %bitcast.9), custom_call_target="tpu_custom_call" | custom-call | tf_op jit(solution)/shard_map/pallas_call | solution.py:387
  41.0 24.1 %all_to_all.28 = f32[32,32,128]{2,1,0:T(8,128)S(1)} all-to-all(f32[32,32,128]{2,1,0:T(8,128)S(1)} %bitcast.13), channel_id=1, replica_groups=mesh['tm'=32,'azi'=2,'rad'=4] {'tm'}, dimensions={0} | all-to-all | bytes 1048576 | tf_op jit(solution)/shard_map/all_to_all | solution.py:414
  65.1 0.9 shard_map.87
  66.0 28.2 %all_to_all.29 = f32[256,1,384]{2,1,0:T(1,128)S(1)} all-to-all(f32[256,1,384]{2,1,0:T(1,128)S(1)} %bitcast.12), channel_id=1, replica_groups=mesh['tm'=32,'azi'=2,'rad'=4] {'tm','azi','rad'}, dimensions={0} | all-to-all | bytes 786432 | tf_op jit(solution)/shard_map/all_to_all | solution.py:417
  94.2 0.9 shard_map.88
Async XLA Ops:
  3.3 29.1 %copy-start = (f32[3]{0:T(128)S(1)}, f32[3]{0:T(128)}, u32[]{:S(2)}) copy-start(f32[3]{0:T(128)} %coef.3) | copy-start | bytes 40

commit v5 on v4

--- a/solution.py
+++ b/solution.py
@@ -62,7 +62,7 @@
     return (group % 2) * RADS + group // 2
 
 
-def pack_kernel(start_at, target_at, cond_at, material_at, current_at, out, start, target, cond, material, current, sems):
+def pack_kernel(start_at, target_at, cond_at, material_at, current_at, out_at, start, target, cond, material, current, out, sems, sent):
     pairs = ((start_at, start), (material_at, material), (cond_at, cond), (current_at, current), (target_at, target))
     copies = [pltpu.make_async_copy(src, dst, sems.at[k]) for k, (src, dst) in enumerate(pairs)]
     for copy in copies:
@@ -75,25 +75,39 @@
         edge = jnp.zeros((HALO, NZ), jnp.float32)
         padded = jnp.concatenate([edge, turned(read, half), edge], axis=0)
         for j in range(BLOCKS):
-            out[pl.ds(j * ROWS + field * GROUP + half * WIN, WIN), :] = padded[ZB * j : ZB * j + WIN]
+            out[j, pl.ds(field * GROUP + half * WIN, WIN), :] = padded[ZB * j : ZB * j + WIN]
+
+    sends = []
+
+    def send(field, size):
+        rows = pl.ds(field * GROUP, size)
+        sends.append(pltpu.make_async_copy(out.at[:, rows, :], out_at.at[:, rows, :], sent.at[field]))
+        sends[-1].start()
 
     copies[0].wait()
     for half in range(2):
         put(0, half, lambda r, q: start[r, q, :])
+    send(0, GROUP)
     copies[1].wait()
     for half in range(2):
         put(1, half, lambda r, q: jnp.where(material[r, q, :] == 1, 1.0, 0.0))
+    send(1, GROUP)
     copies[2].wait()
     for half in range(2):
         put(2, half, lambda r, q: cond[r, q, :])
+    send(2, GROUP)
     copies[3].wait()
     for half in range(2):
         put(3, half, lambda r, q: jnp.where(material[r, q, :] == 2, current[r, q, :], 0.0))
+    send(3, GROUP)
     copies[4].wait()
     for half in range(2):
         flat = turned(lambda r, q: target[r, q, :], half)
         for j in range(BLOCKS):
-            out[pl.ds(j * ROWS + FIELDS * GROUP + half * ZB, ZB), :] = flat[ZB * j : ZB * (j + 1)]
+            out[j, pl.ds(FIELDS * GROUP + half * ZB, ZB), :] = flat[ZB * j : ZB * (j + 1)]
+    send(4, 2 * ZB)
+    for copy in sends:
+        copy.wait()
 
 
 def fine_kernel(coef, got, out, static, xa, xb, rho, iron, cond, source, sat, step_d, base, a_rp, a_rm, a_ap, a_am, a_zp, a_zm):
@@ -211,20 +225,21 @@
         rows = pl.ds(PAD + z0, nz)
         own = pl.ds(z0, nz)
         lane = lax.broadcasted_iota(jnp.int32, (nz, NZ), 1)
+        below = [x[edged(q, -1), rows, :] for q in range(2)]
+        middle = [x[edged(q, 0), rows, :] for q in range(2)]
         for s in range(INNER):
+            above = [x[edged(q, s + 1), rows, :] for q in range(2)]
             for q in range(2):
                 i, at = q * INNER + s, edged(q, s)
-                centre = x[at, rows, :]
-                beside = x[edged(1 - q, s), rows, :]
+                centre, beside = middle[q], middle[1 - q]
                 rolled = pltpu.roll(beside, NZ - 1 if q else 1, 1)
                 up, down = (rolled, beside) if q else (beside, rolled)
                 total = base[i, own, :] - centre
-                total = total + a_rp[i, own, :] * x[at + 1, rows, :]
-                total = total + a_rm[i, own, :] * x[at - 1, rows, :]
-                total = total + a_ap[i, own, :] * up
-                total = total + a_am[i, own, :] * down
+                total = total + a_rp[i, own, :] * above[q]
+                total = total + a_rm[i, own, :] * below[q]
                 total = total + a_zp[i, own, :] * x[at, pl.ds(PAD + z0 + 1, nz), :]
                 total = total + a_zm[i, own, :] * x[at, pl.ds(PAD + z0 - 1, nz), :]
+                total = total + (a_ap[i, own, :] * up + a_am[i, own, :] * down)
                 change = beta * total
                 if alpha is not None:
                     change = change + alpha * step_d[i, own, :]
@@ -238,6 +253,7 @@
                 if s == INNER - 1:
                     last = pltpu.roll(value, 16, 1)
                     fresh[edged(q, -1), rows, :] = jnp.where(lane < 16, 0.0, last)
+            below, middle = middle, above
 
     theta = 0.5 * (UPPER_EDGE + LOWER_EDGE)
     delta = 0.5 * (UPPER_EDGE - LOWER_EDGE)
@@ -405,10 +421,12 @@
     field = pltpu.VMEM((RB, AB, NZ), jnp.float32)
     packed = call(
         pack_kernel,
-        shape(BLOCKS * ROWS, NZ),
+        shape(BLOCKS, ROWS, NZ),
         "hhhhh",
-        [field, field, field, pltpu.VMEM((RB, AB, NZ), jnp.int32), field, pltpu.SemaphoreType.DMA((5,))],
-    )(start_states[0], target[0], conductivity, material, current)
+        [field, field, field, pltpu.VMEM((RB, AB, NZ), jnp.int32), field, pltpu.VMEM((BLOCKS, ROWS, NZ), jnp.float32)]
+        + [pltpu.SemaphoreType.DMA((5,))] * 2,
+        out_specs=pl.BlockSpec(memory_space=pltpu.HBM),
+    )(start_states[0], target[0], conductivity, material, current).reshape(BLOCKS * ROWS, NZ)
     whole = lax.all_to_all(packed, ("azi", "rad"), 0, 0, tiled=True)
     fine, static = solve(bh_coef, whole)
     slices = lax.all_to_all(fine, "tm", 0, 0, tiled=True)

time: 95.3 us -> 94.5 us (level)
  no operation moved by 1% of the time
where the time goes in v5:
time: 94.5 us; the launch traced here: 94.3 us
  blocking collectives  81.4 us (86%)
  Pallas kernels  12.3 us (13%)
    all_to_all x1, blocking collectives, local(): whole = lax.all_to_all(packed, ('azi', 'rad'), 0, 0, tiled=True)  29.1 us
    all_to_all x1, blocking collectives, local(): lax.all_to_all(chained.reshape(SLICES * BLOCKS, 1, 3 * NZ), ('tm', 'azi',...  28.2 us
    all_to_all x1, blocking collectives, local(): slices = lax.all_to_all(fine, 'tm', 0, 0, tiled=True)  24.1 us
    pallas_call x1, Pallas kernels, solve(): call(fine_kernel, (shape(SLICES * 32, NZ), shape(16, NZ)), 'sv', [pltpu.V...  8.18 us
    pallas_call x1, Pallas kernels, local(): call(pack_kernel, shape(BLOCKS, ROWS, NZ), 'hhhhh', [field, field, field,...  2.31 us

profile of v5, /device:TPU:1, one launch (start us, length us, event | category | flops | bytes accessed | tf_op | source)
XLA Modules:
  0.0 94.3 jit_solution(6280541404930797486)
XLA Ops:
  0.6 2.3 %shard_map.85 = f32[8,416,128]{2,1,0:T(8,128)} custom-call(f32[16,16,128]{2,1,0:T(8,128)} %bitcast.13, f32[16,16,128]{2,1,0:T(8,128)} %bitcast.14, f32[16,16,128]{2,1,0:T(8,128)} %cond_at.1, s32[16,16,128]{2,1,0:T(8,128)} %material_at.1, f32[16,16,128]{2,1,0:T(8,128)} %current_at.1), custom_call_target="tpu_custom_call" | custom-call | tf_op jit(solution)/shard_map/pallas_call | solution.py:422
  2.9 0.0 copy-start
  3.0 29.1 %all_to_all.24 = f32[8,416,128]{2,1,0:T(8,128)S(1)} all-to-all(f32[8,416,128]{2,1,0:T(8,128)} %shard_map.85), channel_id=1, replica_groups=mesh['tm'=32,'azi'=2,'rad'=4] {'azi','rad'}, dimensions={0} | all-to-all | bytes 3407872 | tf_op jit(solution)/shard_map/all_to_all | solution.py:430
  32.0 0.0 copy-done
  32.0 8.2 %shard_map.86 = (f32[1024,128]{1,0:T(8,128)S(1)}, f32[16,128]{1,0:T(8,128)S(1)}) custom-call(f32[3]{0:T(128)S(1)} %copy-done, f32[3328,128]{1,0:T(8,128)S(1)} %bitcast.8), custom_call_target="tpu_custom_call" | custom-call | tf_op jit(solution)/shard_map/pallas_call | solution.py:403
  40.2 24.1 %all_to_all.25 = f32[32,32,128]{2,1,0:T(8,128)S(1)} all-to-all(f32[32,32,128]{2,1,0:T(8,128)S(1)} %bitcast.12), channel_id=1, replica_groups=mesh['tm'=32,'azi'=2,'rad'=4] {'tm'}, dimensions={0} | all-to-all | bytes 1048576 | tf_op jit(solution)/shard_map/all_to_all | solution.py:432
  64.3 0.9 shard_map.87
  65.2 28.2 %all_to_all.26 = f32[256,1,384]{2,1,0:T(1,128)S(1)} all-to-all(f32[256,1,384]{2,1,0:T(1,128)S(1)} %bitcast.11), channel_id=1, replica_groups=mesh['tm'=32,'azi'=2,'rad'=4] {'tm','azi','rad'}, dimensions={0} | all-to-all | bytes 786432 | tf_op jit(solution)/shard_map/all_to_all | solution.py:435
  93.4 0.9 shard_map.88
Async XLA Ops:
  2.9 29.1 %copy-start = (f32[3]{0:T(128)S(1)}, f32[3]{0:T(128)}, u32[]{:S(2)}) copy-start(f32[3]{0:T(128)} %coef.3) | copy-start | bytes 40

commit v6 on v5

--- a/solution.py
+++ b/solution.py
@@ -59,7 +59,7 @@
 
 
 def block_of(group):
-    return (group % 2) * RADS + group // 2
+    return group
 
 
 def pack_kernel(start_at, target_at, cond_at, material_at, current_at, out_at, start, target, cond, material, current, out, sems, sent):
@@ -112,7 +112,7 @@
 
 def fine_kernel(coef, got, out, static, xa, xb, rho, iron, cond, source, sat, step_d, base, a_rp, a_rm, a_ap, a_am, a_zp, a_zm):
     b0, b1, b2 = coef[0], coef[1], coef[2]
-    me = lax.axis_index("azi") * RADS + lax.axis_index("rad")
+    me = lax.axis_index("rad") * 2 + lax.axis_index("azi")
     slot = lax.axis_index("tm")
 
     def edged(q, s):
@@ -427,13 +427,13 @@
         + [pltpu.SemaphoreType.DMA((5,))] * 2,
         out_specs=pl.BlockSpec(memory_space=pltpu.HBM),
     )(start_states[0], target[0], conductivity, material, current).reshape(BLOCKS * ROWS, NZ)
-    whole = lax.all_to_all(packed, ("azi", "rad"), 0, 0, tiled=True)
+    whole = lax.all_to_all(packed, ("rad", "azi"), 0, 0, tiled=True)
     fine, static = solve(bh_coef, whole)
     slices = lax.all_to_all(fine, "tm", 0, 0, tiled=True)
     line = pltpu.VMEM((SLICES, 8, NZ), jnp.float32)
     chained = call(chain_kernel, shape(SLICES * 24, NZ), "svv", [line] * 4)(bh_coef, slices, static)
     results = lax.all_to_all(
-        chained.reshape(SLICES * BLOCKS, 1, 3 * NZ), ("tm", "azi", "rad"), 0, 0, tiled=True
+        chained.reshape(SLICES * BLOCKS, 1, 3 * NZ), ("tm", "rad", "azi"), 0, 0, tiled=True
     ).reshape(SLICES * 24, NZ)
     end, grad, coef_grad = call(
         unpack_kernel,

time: 94.5 us -> 94.4 us (level)
  no operation moved by 1% of the time
where the time goes in v6:
time: 94.4 us; the launch traced here: 94.2 us
  blocking collectives  81.3 us (86%)
  Pallas kernels  12.3 us (13%)
    all_to_all x1, blocking collectives, local(): whole = lax.all_to_all(packed, ('rad', 'azi'), 0, 0, tiled=True)  28.9 us
    all_to_all x1, blocking collectives, local(): lax.all_to_all(chained.reshape(SLICES * BLOCKS, 1, 3 * NZ), ('tm', 'rad',...  28.3 us
    all_to_all x1, blocking collectives, local(): slices = lax.all_to_all(fine, 'tm', 0, 0, tiled=True)  24.1 us
    pallas_call x1, Pallas kernels, solve(): call(fine_kernel, (shape(SLICES * 32, NZ), shape(16, NZ)), 'sv', [pltpu.V...  8.18 us
    pallas_call x1, Pallas kernels, local(): call(pack_kernel, shape(BLOCKS, ROWS, NZ), 'hhhhh', [field, field, field,...  2.31 us

profile of v6, /device:TPU:1, one launch (start us, length us, event | category | flops | bytes accessed | tf_op | source)
XLA Modules:
  0.0 94.2 jit_solution(1424226407385099619)
XLA Ops:
  0.6 2.3 %shard_map.85 = f32[8,416,128]{2,1,0:T(8,128)} custom-call(f32[16,16,128]{2,1,0:T(8,128)} %bitcast.13, f32[16,16,128]{2,1,0:T(8,128)} %bitcast.14, f32[16,16,128]{2,1,0:T(8,128)} %cond_at.1, s32[16,16,128]{2,1,0:T(8,128)} %material_at.1, f32[16,16,128]{2,1,0:T(8,128)} %current_at.1), custom_call_target="tpu_custom_call" | custom-call | tf_op jit(solution)/shard_map/pallas_call | solution.py:422
  2.9 0.0 copy-start
  3.0 28.9 %all_to_all.24 = f32[8,416,128]{2,1,0:T(8,128)S(1)} all-to-all(f32[8,416,128]{2,1,0:T(8,128)} %shard_map.85), channel_id=1, replica_groups=mesh['tm'=32,'azi'=2,'rad'=4] {'rad','azi'}, dimensions={0} | all-to-all | bytes 3407872 | tf_op jit(solution)/shard_map/all_to_all | solution.py:430
  31.8 0.0 copy-done
  31.8 8.2 %shard_map.86 = (f32[1024,128]{1,0:T(8,128)S(1)}, f32[16,128]{1,0:T(8,128)S(1)}) custom-call(f32[3]{0:T(128)S(1)} %copy-done, f32[3328,128]{1,0:T(8,128)S(1)} %bitcast.8), custom_call_target="tpu_custom_call" | custom-call | tf_op jit(solution)/shard_map/pallas_call | solution.py:403
  40.0 24.1 %all_to_all.25 = f32[32,32,128]{2,1,0:T(8,128)S(1)} all-to-all(f32[32,32,128]{2,1,0:T(8,128)S(1)} %bitcast.12), channel_id=1, replica_groups=mesh['tm'=32,'azi'=2,'rad'=4] {'tm'}, dimensions={0} | all-to-all | bytes 1048576 | tf_op jit(solution)/shard_map/all_to_all | solution.py:432
  64.1 0.9 shard_map.87
  65.0 28.3 %all_to_all.26 = f32[256,1,384]{2,1,0:T(1,128)S(1)} all-to-all(f32[256,1,384]{2,1,0:T(1,128)S(1)} %bitcast.11), channel_id=1, replica_groups=mesh['tm'=32,'azi'=2,'rad'=4] {'tm','rad','azi'}, dimensions={0} | all-to-all | bytes 786432 | tf_op jit(solution)/shard_map/all_to_all | solution.py:435
  93.3 0.9 shard_map.88
Async XLA Ops:
  2.9 28.9 %copy-start = (f32[3]{0:T(128)S(1)}, f32[3]{0:T(128)}, u32[]{:S(2)}) copy-start(f32[3]{0:T(128)} %coef.3) | copy-start | bytes 40
